TPU v7x, 32 devices: a whole 2x2x4 slice. The times are simulated.
32 devices in a mesh: groups: 2 (over x), dp: 16 (over z, y, core).
Axes of the slice: x: 2, y: 2, z: 4, core: 2. Of those that a mesh axis runs over, the one named last changes fastest.
Arguments:
- hidden_in: bfloat16 [32768, 768], P(('groups', 'dp')), parts along dimension 0, may hold values from -6 to 6
- up_weight: bfloat16 [768, 3072], replicated, may hold values from -0.21875 to 0.21875
- up_bias: float32 [3072], replicated, may hold values from -3 to 3
- down_weight: bfloat16 [3072, 768], replicated, may hold values from -0.109375 to 0.109375
- down_bias: float32 [768], replicated, may hold values from -3 to 3
- norm_gain: float32 [768], replicated, may hold values from 0.1 to 1.9
- norm_shift: float32 [768], replicated, may hold values from -3 to 3
- proj_weight: bfloat16 [768, 128], replicated, may hold values from -0.21875 to 0.21875
- centroids: bfloat16 [65536, 128], P('dp'), may hold values from -0.5 to 0.5
- lengths: int32 [256], P(('groups', 'dp')), parts along dimension 0, may hold values from 1 to 128, 12288 in all
- owners: int32 [32768, 1], P(('groups', 'dp')), parts along dimension 0, may hold values from 0 to 15; in each aligned block of 1024 rows (0 to 1023, 1024 to 2047, ...) at most 128 rows name the same one
- local_ids: int32 [32768], P(('groups', 'dp')), parts along dimension 0, may hold values from 0 to 4095
Outputs:
- residuals: bfloat16 [32768, 128], P(('groups', 'dp')), parts along dimension 0
There are 2 independent parts, one for each index of `groups`. A program takes and returns all parts, laid end to end along the dimension named above; an argument that names none is the same for every part. Nothing has to cross between parts.
Inputs may be any that keep to these rules, and one draw needn't show every extreme that they name: `owners`: in the rows of one device (1024 rows) no owner is named by more than 128 rows, and one owner by exactly 128; every owner is named somewhere. All lengths together sum to 12288.
All inputs are finite; a program needn't handle non-finite values. No bound on the sum of `lengths` on one device may be relied on, other than what follows from the above.
Results may differ from a plain program's by a relative error of at most 0.0051.
Values may be sent and summed in bfloat16 or wider, within the bound.
No kernel may reach another device: no remote copies, remote signals or barrier semaphores. Data moves between devices by JAX's collectives and lax.ppermute only.
A program may use at most 64 MiB of HBM per device.

v0:
```python
import jax
import jax.numpy as jnp
from jax import lax
from jax.sharding import PartitionSpec as P

LEN = 128


def encode_rows(
    rows, up_weight, up_bias, down_weight, down_bias, norm_gain, norm_shift, proj_weight
):
    up_proj = jnp.dot(rows, up_weight, preferred_element_type=jnp.float32) + up_bias
    activated = jax.nn.gelu(up_proj, approximate=False).astype(jnp.bfloat16)
    ffn_out = (
        jnp.dot(activated, down_weight, preferred_element_type=jnp.float32)
        + down_bias
        + rows.astype(jnp.float32)
    )
    center = jnp.mean(ffn_out, axis=1, keepdims=True)
    spread = jnp.mean((ffn_out - center) ** 2, axis=1, keepdims=True)
    normed = ((ffn_out - center) / jnp.sqrt(spread + 1e-05) * norm_gain + norm_shift).astype(
        jnp.bfloat16
    )
    projected = jnp.dot(normed, proj_weight, preferred_element_type=jnp.float32)
    return (
        projected / jnp.sqrt(jnp.sum(projected * projected, axis=1, keepdims=True) + 1e-06)
    ).astype(jnp.bfloat16)


def body(
    hidden_in,
    up_weight,
    up_bias,
    down_weight,
    down_bias,
    norm_gain,
    norm_shift,
    proj_weight,
    centroids,
    lengths,
    owners,
    local_ids,
):
    n_devices = lax.axis_size("dp")
    token_rows = hidden_in.shape[0]
    width_out = proj_weight.shape[1]
    position = jnp.arange(token_rows, dtype=jnp.int32) % LEN
    passage_len = jnp.repeat(lengths, LEN)
    live_flag = position < passage_len
    alive = live_flag[:, None]
    embedded = encode_rows(
        hidden_in, up_weight, up_bias, down_weight, down_bias, norm_gain, norm_shift, proj_weight
    )
    capacity = max(2, 2 * token_rows // n_devices)
    owner_col = owners[:, 0]
    one_hot = (owner_col[:, None] == jnp.arange(n_devices, dtype=jnp.int32)[None, :]).astype(
        jnp.int32
    )
    earlier = jnp.cumsum(one_hot, axis=0) - one_hot
    slot_number = jnp.sum(earlier * one_hot, axis=1)
    slot_index = owner_col * capacity + slot_number
    slot_ids = (
        jnp.zeros((n_devices * capacity,), jnp.int32)
        .at[slot_index]
        .set(local_ids)
        .reshape(n_devices, capacity)
    )
    outgoing = (
        jnp.zeros((n_devices * capacity, width_out), jnp.bfloat16)
        .at[slot_index]
        .set(embedded)
        .reshape(n_devices, capacity, width_out)
    )
    arrived, arrived_ids = (
        lax.all_to_all(outgoing, "dp", split_axis=0, concat_axis=0, tiled=True),
        lax.all_to_all(slot_ids, "dp", split_axis=0, concat_axis=0, tiled=True),
    )
    centers = centroids[arrived_ids]
    difference = arrived.astype(jnp.float32) - centers.astype(jnp.float32)
    scale = jnp.sqrt(jnp.sum(difference * difference, axis=2, keepdims=True) + 1e-06)
    answers = (difference / scale).astype(jnp.bfloat16)
    returned = lax.all_to_all(answers, "dp", split_axis=0, concat_axis=0, tiled=True)
    result = returned.reshape(n_devices * capacity, width_out)[slot_index].astype(jnp.float32)
    return jnp.where(alive, result, 0.0).astype(jnp.bfloat16)


def solution(mesh):
    in_specs = (
        P(("groups", "dp"), None),
        P(),
        P(),
        P(),
        P(),
        P(),
        P(),
        P(),
        P("dp", None),
        P(("groups", "dp")),
        P(("groups", "dp"), None),
        P(("groups", "dp")),
    )
    out_specs = P(("groups", "dp"), None)
    return jax.shard_map(body, mesh=mesh, in_specs=in_specs, out_specs=out_specs, check_vma=False)
```

profile of v0, /device:TPU:0, one launch (start us, length us, event | category | flops | bytes accessed | tf_op | source)
XLA Modules:
  0.0 114.2 jit_solution(14693275446398086039)
XLA Ops:
  0.0 0.0 copy-start
  0.0 0.8 fusion.20
  0.8 4.5 %reduce-window.6 = s32[16,8,128]{2,1,0:T(8,128)S(1)} reduce-window(s32[16,8,128]{2,1,0:T(8,128)S(1)} %fusion.20, s32[]{:T(128)} %constant.40.clone.1), window={size=1x1x128 pad=0_0x0_0x127_0}, to_apply=%region_0.1 | reduce-window | flops 2080768 | bytes 131076 | tf_op jit(solution)/shard_map/reduce-window
  5.3 0.1 slice.12
  5.4 0.1 copy.16
  5.5 0.1 copy.17
  5.6 0.1 broadcast_add_fusion
  5.7 0.7 fusion.19
  6.4 0.7 compare_select_fusion
  7.1 5.0 %scatter_custom_fusion.1 = s32[2048]{0:T(1024)} fusion(s32[1024]{0:T(1024)S(1)} %bitcast.55, s32[1024]{0:T(1024)} %param.23, s32[]{:T(128)} %constant.40.clone.1), kind=kCustom, calls=%fused_computation.51 | custom fusion | bytes 8704 | tf_op jit(solution)/shard_map/scatter | solution.py:65
  12.2 7.4 %all-to-all-start.1 = ((s32[16,1,128]{2,1,0:T(1,128)}), s32[16,1,128]{2,1,0:T(1,128)S(1)}, u32[]{:S(2)}, u32[]{:S(2)}) async-start(s32[16,1,128]{2,1,0:T(1,128)} %bitcast.8), calls=%async_computation.1 | async-start | bytes 16384 | tf_op jit(solution)/shard_map/all_to_all | solution.py:76
  19.6 1.7 %copy.18 = bf16[1024,768]{0,1:T(8,128)(2,1)S(1)} copy(bf16[1024,768]{1,0:T(8,128)(2,1)} %param.12) | data formatting | bytes 3145728 | tf_op args[0]
  21.3 0.0 copy-start.1
  21.3 0.0 copy-start.2
  21.3 0.0 copy-start.3
  21.3 38.9 %fusion.59 = (f32[1024]{0:T(1024)S(1)}, f32[1024,768]{0,1:T(8,128)}) fusion(bf16[1024,768]{0,1:T(8,128)(2,1)S(1)} %copy.18, f32[768]{0:T(1024)} %param.16, bf16[3072,768]{1,0:T(8,128)(2,1)} %param.15, f32[3072]{0:T(1024)} %param.14, bf16[1024,768]{1,0:T(8,128)(2,1)} %param.12, bf16[768,3072]{1,0:T(8,128)(2,1)} %param.13), kind=kOutput, calls=%fused_computation.91 | convolution fusion | flops 9874439168 | bytes 15748096 | tf_op jit(solution)/shard_map/dot_general | solution.py:15
  60.3 2.3 %multiply_reduce_fusion = f32[1024]{0:T(1024)S(1)} fusion(f32[1024,768]{0,1:T(8,128)} %get-tuple-element.6, f32[1024]{0:T(1024)S(1)} %broadcast_multiply_fusion), kind=kLoop, calls=%fused_computation.25 | loop fusion | flops 2358272 | bytes 3153920 | tf_op jit(solution)/shard_map/reduce_sum | solution.py:20
  62.5 0.0 copy-done.1
  62.5 0.0 copy-done.2
  62.5 0.0 copy-done.3
  62.5 2.6 %multiply_reduce_fusion.2 = (f32[1024]{0:T(1024)S(1)}, f32[1024,128]{0,1:T(8,128)S(1)}) fusion(bf16[768,128]{1,0:T(8,128)(2,1)S(1)} %copy-done.1, f32[1024,768]{0,1:T(8,128)} %get-tuple-element.6, f32[768]{0:T(1024)S(1)} %copy-done.2, f32[768]{0:T(1024)S(1)} %copy-done.3, f32[1024]{0:T(1024)S(1)} %add_sqrt_fusion.2, f32[1024]{0:T(1024)S(1)} %broadcast_multiply_fusion), kind=kOutput, calls=%fused_computation.33 | convolution fusion | flops 205519872 | bytes 3885056 | tf_op jit(solution)/shard_map/dot_general | solution.py:24
  65.3 0.2 copy.19
  65.4 4.0 %scatter_custom_fusion = bf16[2048,128]{1,0:T(8,128)(2,1)} fusion(s32[1024]{0:T(1024)S(1)} %bitcast.56, bf16[1024,128]{1,0:T(8,128)(2,1)S(1)} %copy.19, bf16[]{:T(256)} %constant.42.clone.1), kind=kCustom, calls=%fused_computation.34 | custom fusion | bytes 524290 | tf_op jit(solution)/shard_map/scatter | solution.py:71
  69.4 0.0 all-to-all-done.1
  69.4 0.0 copy-start.4
  69.4 6.1 %all-to-all-start = ((bf16[16,128,128]{2,1,0:T(8,128)(2,1)}), bf16[16,128,128]{2,1,0:T(8,128)(2,1)S(1)}, u32[]{:S(2)}, u32[]{:S(2)}) async-start(bf16[16,128,128]{2,1,0:T(8,128)(2,1)} %bitcast.7), calls=%async_computation | async-start | bytes 1048576 | tf_op jit(solution)/shard_map/all_to_all | solution.py:75
  75.6 0.0 copy-done
  75.6 6.2 %gather_fusion = bf16[2048,128]{1,0:T(8,128)(2,1)S(1)} fusion(bf16[4096,128]{1,0:T(8,128)(2,1)S(1)} %copy-done, s32[2048]{0:T(1024)S(1)} %fusion.22), kind=kCustom, calls=%fused_computation | custom fusion | bytes 1056768 | tf_op jit(solution)/shard_map/gather | solution.py:78
  81.8 8.3 %all-to-all-done = bf16[16,128,128]{2,1,0:T(8,128)(2,1)S(1)} async-done(((bf16[16,128,128]{2,1,0:T(8,128)(2,1)}), bf16[16,128,128]{2,1,0:T(8,128)(2,1)S(1)}, u32[]{:S(2)}, u32[]{:S(2)}) %all-to-all-start) | async-done | bytes 524320 | tf_op jit(solution)/shard_map/all_to_all | solution.py:75
  90.0 0.4 multiply_reduce_fusion.1
  90.4 1.1 divide_convert_fusion
  91.5 4.1 %all-to-all-start.2 = ((bf16[16,128,128]{2,1,0:T(8,128)(2,1)}), bf16[16,128,128]{2,1,0:T(8,128)(2,1)S(1)}, u32[]{:S(2)}, u32[]{:S(2)}) async-start(bf16[16,128,128]{2,1,0:T(8,128)(2,1)} %divide_convert_fusion), calls=%async_computation.2 | async-start | bytes 1048576 | tf_op jit(solution)/shard_map/all_to_all | solution.py:82
  95.6 0.0 copy-done.4
  95.6 0.1 fusion.23
  95.7 14.4 %all-to-all-done.2 = bf16[16,128,128]{2,1,0:T(8,128)(2,1)S(1)} async-done(((bf16[16,128,128]{2,1,0:T(8,128)(2,1)}), bf16[16,128,128]{2,1,0:T(8,128)(2,1)S(1)}, u32[]{:S(2)}, u32[]{:S(2)}) %all-to-all-start.2) | async-done | bytes 524320 | tf_op jit(solution)/shard_map/all_to_all | solution.py:82
  110.1 3.2 %gather_fusion.1 = bf16[1024,128]{1,0:T(8,128)(2,1)S(1)} fusion(bf16[2048,128]{1,0:T(8,128)(2,1)S(1)} %bitcast.47, s32[1024]{0:T(1024)S(1)} %broadcast_clamp_fusion), kind=kCustom, calls=%fused_computation.1 | custom fusion | bytes 528384 | tf_op jit(solution)/shard_map/gather | solution.py:83
  113.3 0.9 select_convert_fusion
  (9 shorter events, 0.1 us)
Async XLA Ops:
  0.0 75.6 %copy-start = (bf16[4096,128]{1,0:T(8,128)(2,1)S(1)}, bf16[4096,128]{1,0:T(8,128)(2,1)}, u32[]{:S(2)}) copy-start(bf16[4096,128]{1,0:T(8,128)(2,1)} %param.20) | copy-start | bytes 3145732
  12.2 57.2 %all-to-all-start.1 = ((s32[16,1,128]{2,1,0:T(1,128)}), s32[16,1,128]{2,1,0:T(1,128)S(1)}, u32[]{:S(2)}, u32[]{:S(2)}) async-start(s32[16,1,128]{2,1,0:T(1,128)} %bitcast.8), calls=%async_computation.1 | async-start | bytes 16384 | tf_op jit(solution)/shard_map/all_to_all | solution.py:76
  21.3 41.2 %copy-start.1 = (bf16[768,128]{1,0:T(8,128)(2,1)S(1)}, bf16[768,128]{1,0:T(8,128)(2,1)}, u32[]{:S(2)}) copy-start(bf16[768,128]{1,0:T(8,128)(2,1)} %param.19) | copy-start | bytes 589828
  21.3 41.2 %copy-start.2 = (f32[768]{0:T(1024)S(1)}, f32[768]{0:T(1024)}, u32[]{:S(2)}) copy-start(f32[768]{0:T(1024)} %param.18) | copy-start | bytes 9220
  21.3 41.2 %copy-start.3 = (f32[768]{0:T(1024)S(1)}, f32[768]{0:T(1024)}, u32[]{:S(2)}) copy-start(f32[768]{0:T(1024)} %param.17) | copy-start | bytes 9220
  69.4 26.2 %copy-start.4 = (s32[8]{0:T(128)S(1)}, s32[8]{0:T(128)}, u32[]{:S(2)}) copy-start(s32[8]{0:T(128)} %param.21) | copy-start | bytes 100
  69.4 20.6 %all-to-all-start = ((bf16[16,128,128]{2,1,0:T(8,128)(2,1)}), bf16[16,128,128]{2,1,0:T(8,128)(2,1)S(1)}, u32[]{:S(2)}, u32[]{:S(2)}) async-start(bf16[16,128,128]{2,1,0:T(8,128)(2,1)} %bitcast.7), calls=%async_computation | async-start | bytes 1048576 | tf_op jit(solution)/shard_map/all_to_all | solution.py:75
  91.5 18.6 %all-to-all-start.2 = ((bf16[16,128,128]{2,1,0:T(8,128)(2,1)}), bf16[16,128,128]{2,1,0:T(8,128)(2,1)S(1)}, u32[]{:S(2)}, u32[]{:S(2)}) async-start(bf16[16,128,128]{2,1,0:T(8,128)(2,1)} %divide_convert_fusion), calls=%async_computation.2 | async-start | bytes 1048576 | tf_op jit(solution)/shard_map/all_to_all | solution.py:82
where the time goes:
time: 115 us; the launch traced here: 114 us
  matrix products  41.6 us (36%)
  waiting for transfers between devices  22.6 us (20%)
  local copies, waits for them, and re-layouts  20.6 us (18%)
  starting transfers between devices  17.6 us (15%)
  other arithmetic  11.6 us (10%)
    dot_general x1, matrix products, encode_rows(): jnp.dot(activated, down_weight, preferred_element_type=jnp.float32)  38.9 us
    all_to_all x1, waiting for transfers between devices, body(): lax.all_to_all(answers, 'dp', split_axis=0, concat_axis=0, tiled=True)  14.4 us
    all_to_all x1, waiting for transfers between devices, body(): lax.all_to_all(outgoing, 'dp', split_axis=0, concat_axis=0, tiled=True)  8.26 us
    all_to_all x1, starting transfers between devices, body(): lax.all_to_all(slot_ids, 'dp', split_axis=0, concat_axis=0, tiled=True)  7.39 us
    gather x1, local copies, waits for them, and re-layouts, body(): centers = centroids[arrived_ids]  6.18 us
    all_to_all x1, starting transfers between devices, body(): lax.all_to_all(outgoing, 'dp', split_axis=0, concat_axis=0, tiled=True)  6.14 us
    scatter x1, local copies, waits for them, and re-layouts, body(): slot_ids = jnp.zeros((n_devices * capacity,), jnp.int32).at[slot_index].s...  5.04 us
    another operation x3, other arithmetic  4.61 us
  transfers between devices with their start and end apart: 3, of which 2 were waited for; matrix products, arithmetic and copies ran while one was open for 49% of the time, Pallas kernels for 0%

commit v1 on v0

v1 whole, which is shorter than its diff:
```python
import functools

import jax
import jax.numpy as jnp
from jax import lax
from jax.experimental import pallas as pl
from jax.experimental.pallas import tpu as pltpu
from jax.sharding import PartitionSpec as P

LEN = 128
LANES = 128
LOW = 64
VMEM_BYTES = 48 * 2**20
VMEM = pl.BlockSpec(memory_space=pltpu.VMEM)
SMEM = pl.BlockSpec(memory_space=pltpu.SMEM)
HBM = pl.BlockSpec(memory_space=pl.ANY)


def plan_kernel(owners_ref, ids_ref, slots_ref, asked_ref):
    n_owners, capacity = asked_ref.shape
    n_rows = owners_ref.shape[0]
    owner_iota = lax.broadcasted_iota(jnp.int32, (n_owners, LANES), 0)
    slot_iota = lax.broadcasted_iota(jnp.int32, (capacity, LANES), 0)
    before = lax.broadcasted_iota(jnp.int32, (LANES, LANES), 0) < lax.broadcasted_iota(
        jnp.int32, (LANES, LANES), 1
    )
    counter = jnp.concatenate(
        [before.astype(jnp.float32), jnp.ones((LANES, LANES), jnp.float32)], axis=1
    ).astype(jnp.bfloat16)
    named = jnp.zeros((n_owners, LANES), jnp.float32)
    high = jnp.zeros((n_owners, capacity), jnp.float32)
    low = jnp.zeros((n_owners, capacity), jnp.float32)
    for row in range(n_rows):
        owner_row = owners_ref[row : row + 1, :]
        ids_row = ids_ref[row : row + 1, :]
        hot = (owner_iota == owner_row).astype(jnp.float32)
        counts = jnp.dot(hot.astype(jnp.bfloat16), counter, preferred_element_type=jnp.float32)
        slot = jnp.sum(hot * (counts[:, :LANES] + named), axis=0, keepdims=True).astype(jnp.int32)
        named = named + counts[:, LANES:]
        slots_ref[row : row + 1, :] = owner_row * capacity + slot
        placed = (slot_iota == slot).astype(jnp.float32).astype(jnp.bfloat16)
        parts = jnp.concatenate(
            [
                hot * (ids_row // LOW).astype(jnp.float32),
                hot * (ids_row % LOW).astype(jnp.float32),
            ],
            axis=0,
        ).astype(jnp.bfloat16)
        both = lax.dot_general(
            parts, placed, (((1,), (1,)), ((), ())), preferred_element_type=jnp.float32
        )
        high = high + both[:n_owners]
        low = low + both[n_owners:]
    asked_ref[...] = high.astype(jnp.int32) * LOW + low.astype(jnp.int32)


def plan(owners, local_ids, n_owners, capacity):
    rows = owners.shape[0]
    return pl.pallas_call(
        plan_kernel,
        in_specs=[VMEM, VMEM],
        out_specs=[VMEM, VMEM],
        out_shape=[
            jax.ShapeDtypeStruct((rows, LANES), jnp.int32),
            jax.ShapeDtypeStruct((n_owners, capacity), jnp.int32),
        ],
        name="plan",
    )(owners, local_ids)


def gather_kernel(asked_ref, table_ref, out_ref, table_f32, out_f32):
    n_owners, capacity = asked_ref.shape
    table_f32[...] = table_ref[...].astype(jnp.float32)

    def step(owner, carry):
        for slot in range(capacity):
            row = asked_ref[owner, slot]
            out_f32[pl.ds(owner * capacity + slot, 1), :] = table_f32[pl.ds(row, 1), :]
        return carry

    lax.fori_loop(0, n_owners, step, 0)
    out_ref[...] = out_f32[...].astype(jnp.bfloat16)


def gather_rows(asked, table):
    rows = asked.shape[0] * asked.shape[1]
    width = table.shape[1]
    return pl.pallas_call(
        gather_kernel,
        in_specs=[SMEM, VMEM],
        out_specs=VMEM,
        out_shape=jax.ShapeDtypeStruct((rows, width), jnp.bfloat16),
        scratch_shapes=[
            pltpu.VMEM(table.shape, jnp.float32),
            pltpu.VMEM((rows, width), jnp.float32),
        ],
        compiler_params=pltpu.CompilerParams(vmem_limit_bytes=VMEM_BYTES),
        name="gather_rows",
    )(asked, table)


def finish_kernel(slots_ref, lengths_ref, first_ref, second_ref, centers_ref, out_ref, centers_f32, mine):
    centers_f32[...] = centers_ref[...].astype(jnp.float32)
    n_passages = out_ref.shape[0] // LEN
    split = first_ref.shape[0] // LEN

    def step(passage, carry):
        for position in range(LEN):
            row = slots_ref[passage, position]
            mine[pl.ds(passage * LEN + position, 1), :] = centers_f32[pl.ds(row, 1), :]
        return carry

    lax.fori_loop(0, n_passages, step, 0)
    position = lax.broadcasted_iota(jnp.int32, (LEN, 1), 0)
    for passage in range(n_passages):
        at = slice(passage * LEN, (passage + 1) * LEN)
        if passage < split:
            embedded = first_ref[at, :]
        else:
            embedded = second_ref[(passage - split) * LEN : (passage - split + 1) * LEN, :]
        difference = embedded.astype(jnp.float32) - mine[at, :]
        total = jnp.sum(difference * difference, axis=1, keepdims=True)
        result = difference * lax.rsqrt(total + 1e-06)
        alive = position < lengths_ref[passage]
        out_ref[at, :] = jnp.where(alive, result, 0.0).astype(jnp.bfloat16)


def finish(slots, lengths, first, second, centers):
    rows = slots.shape[0] * slots.shape[1]
    width = centers.shape[1]
    return pl.pallas_call(
        finish_kernel,
        in_specs=[SMEM, SMEM, VMEM, VMEM, VMEM],
        out_specs=VMEM,
        out_shape=jax.ShapeDtypeStruct((rows, width), jnp.bfloat16),
        scratch_shapes=[
            pltpu.VMEM(centers.shape, jnp.float32),
            pltpu.VMEM((rows, width), jnp.float32),
        ],
        compiler_params=pltpu.CompilerParams(vmem_limit_bytes=VMEM_BYTES),
        name="finish",
    )(slots, lengths, first, second, centers)


def encode_kernel(
    chunk, rows_ref, up_hbm, up_bias_ref, down_hbm, down_bias_ref, gain_ref, shift_ref, proj_ref,
    out_ref, up_vmem, down_vmem, arrived,
):
    n_chunks = up_vmem.shape[0]

    def up_copy(index):
        return pltpu.make_async_copy(
            up_hbm.at[:, pl.ds(index * chunk, chunk)], up_vmem.at[index], arrived.at[0, index]
        )

    def down_copy(index):
        return pltpu.make_async_copy(
            down_hbm.at[pl.ds(index * chunk, chunk), :], down_vmem.at[index], arrived.at[1, index]
        )

    def tile(first):
        rows = rows_ref[...]
        total = None
        for index in range(n_chunks):
            if first:
                up_copy(index).wait()
            up_proj = (
                jnp.dot(rows, up_vmem[index], preferred_element_type=jnp.float32)
                + up_bias_ref[:, index * chunk : (index + 1) * chunk]
            )
            activated = (0.5 * up_proj * (1.0 + lax.erf(up_proj * 0.7071067811865476))).astype(
                jnp.bfloat16
            )
            if first:
                down_copy(index).wait()
            part = jnp.dot(activated, down_vmem[index], preferred_element_type=jnp.float32)
            total = part if total is None else total + part
        ffn_out = total + down_bias_ref[...] + rows.astype(jnp.float32)
        center = jnp.mean(ffn_out, axis=1, keepdims=True)
        centered = ffn_out - center
        spread = jnp.mean(centered * centered, axis=1, keepdims=True)
        normed = (centered * lax.rsqrt(spread + 1e-05) * gain_ref[...] + shift_ref[...]).astype(
            jnp.bfloat16
        )
        projected = jnp.dot(normed, proj_ref[...], preferred_element_type=jnp.float32)
        size = jnp.sum(projected * projected, axis=1, keepdims=True)
        out_ref[...] = (projected * lax.rsqrt(size + 1e-06)).astype(jnp.bfloat16)

    @pl.when(pl.program_id(0) == 0)
    def _():
        for index in range(n_chunks):
            up_copy(index).start()
            down_copy(index).start()
        tile(True)

    @pl.when(pl.program_id(0) > 0)
    def _():
        tile(False)


def encode(hidden_in, weights, start, rows, tile_rows=256, chunk=768):
    up_weight, up_bias, down_weight, down_bias, norm_gain, norm_shift, proj_weight = weights
    width, hidden = up_weight.shape
    out_width = proj_weight.shape[1]
    n_chunks = hidden // chunk
    start_tile = start // tile_rows

    def whole(array):
        return pl.BlockSpec(array.shape, lambda index: (0, 0))

    return pl.pallas_call(
        functools.partial(encode_kernel, chunk),
        grid=(rows // tile_rows,),
        in_specs=[
            pl.BlockSpec((tile_rows, width), lambda index: (index + start_tile, 0)),
            HBM,
            whole(up_bias),
            HBM,
            whole(down_bias),
            whole(norm_gain),
            whole(norm_shift),
            whole(proj_weight),
        ],
        out_specs=pl.BlockSpec((tile_rows, out_width), lambda index: (index, 0)),
        out_shape=jax.ShapeDtypeStruct((rows, out_width), jnp.bfloat16),
        scratch_shapes=[
            pltpu.VMEM((n_chunks, width, chunk), jnp.bfloat16),
            pltpu.VMEM((n_chunks, chunk, width), jnp.bfloat16),
            pltpu.SemaphoreType.DMA((2, n_chunks)),
        ],
        compiler_params=pltpu.CompilerParams(vmem_limit_bytes=VMEM_BYTES),
        cost_estimate=pl.CostEstimate(
            flops=2 * rows * (2 * width * hidden + width * out_width),
            bytes_accessed=4 * width * hidden + 2 * rows * width,
            transcendentals=0,
        ),
        name="encode",
    )(hidden_in, up_weight, up_bias, down_weight, down_bias, norm_gain, norm_shift, proj_weight)


def body(
    hidden_in, up_weight, up_bias, down_weight, down_bias, norm_gain, norm_shift, proj_weight,
    centroids, lengths, owners, local_ids,
):
    n_devices = lax.axis_size("dp")
    token_rows = hidden_in.shape[0]
    width_out = proj_weight.shape[1]
    capacity = max(2, 2 * token_rows // n_devices)
    weights = (
        up_weight, up_bias[None, :], down_weight, down_bias[None, :],
        norm_gain[None, :], norm_shift[None, :], proj_weight,
    )
    early = token_rows // 4
    slots, asked = plan(
        owners.reshape(-1, LANES), local_ids.reshape(-1, LANES), n_devices, capacity
    )
    arrived = lax.all_to_all(asked, "dp", split_axis=0, concat_axis=0, tiled=True)
    first = encode(hidden_in, weights, 0, early)
    arrived, first = lax.optimization_barrier((arrived, first))
    rows = gather_rows(arrived, centroids)
    hidden_late, rows = lax.optimization_barrier((hidden_in, rows))
    centers = lax.all_to_all(
        rows.reshape(n_devices, capacity, width_out), "dp", split_axis=0, concat_axis=0, tiled=True
    )
    second = encode(hidden_late, weights, early, token_rows - early)
    centers, second = lax.optimization_barrier((centers, second))
    return finish(slots, lengths, first, second, centers.reshape(-1, width_out))


def solution(mesh):
    in_specs = (
        P(("groups", "dp"), None),
        P(),
        P(),
        P(),
        P(),
        P(),
        P(),
        P(),
        P("dp", None),
        P(("groups", "dp")),
        P(("groups", "dp"), None),
        P(("groups", "dp")),
    )
    out_specs = P(("groups", "dp"), None)
    return jax.shard_map(body, mesh=mesh, in_specs=in_specs, out_specs=out_specs, check_vma=False)
```

time: 115 us -> 47.8 us (0.42)
  matrix products: 41.6 us -> 0 us
  Pallas kernels: 0 us -> 27.5 us
  waiting for transfers between devices: 22.6 us -> 1.21 us
  local copies, waits for them, and re-layouts: 20.6 us -> 5.14 us
  other arithmetic: 11.6 us -> 0 us
  starting transfers between devices: 17.6 us -> 13.4 us
    dot_general x2 -> x0, matrix products: 41.6 us -> none  [the longest x1 38.9 us: encode_rows(): jnp.dot(activated, down_weight, preferred_element_type=jnp.float32)]
    pallas_call x0 -> x5, Pallas kernels: none -> 27.5 us  [the longest x2 19.6 us: encode(): pl.pallas_call(functools.partial(encode_kernel, chunk), grid=(rows // til...]
    all_to_all x3 -> x2, waiting for transfers between devices: 22.6 us -> 1.21 us  [the longest x1 1.21 us: body(): lax.all_to_all(rows.reshape(n_devices, capacity, width_out), 'dp', split_...]
    gather x2 -> x0, local copies, waits for them, and re-layouts: 9.38 us -> none  [the longest x1 6.18 us: body(): centers = centroids[arrived_ids]]
    scatter x2 -> x0, local copies, waits for them, and re-layouts: 9.02 us -> none  [the longest x1 5.04 us: body(): slot_ids = jnp.zeros((n_devices * capacity,), jnp.int32).at[slot_index].s...]
    another operation x3 -> x0, other arithmetic: 4.61 us -> none
    all_to_all x3 -> x2, starting transfers between devices: 17.6 us -> 13.4 us  [the longest x1 7.39 us: body(): lax.all_to_all(asked, 'dp', split_axis=0, concat_axis=0, tiled=True)]
    reduce_sum x3 -> x0, other arithmetic: 3.32 us -> none  [the longest x1 2.25 us: encode_rows(): spread = jnp.mean((ffn_out - center) ** 2, axis=1, keepdims=True)]
  transfers between devices with their start and end apart: 3 -> 2, of which waited for: 2 -> 1; matrix products, arithmetic and copies ran while one was open for 49% -> 4% of each run, Pallas kernels for 0% -> 41%
where the time goes in v1:
time: 47.8 us; the launch traced here: 47.3 us
  Pallas kernels  27.5 us (58%)
  starting transfers between devices  13.4 us (28%)
  local copies, waits for them, and re-layouts  5.14 us (11%)
  waiting for transfers between devices  1.21 us (3%)
    pallas_call x2, Pallas kernels, encode(): pl.pallas_call(functools.partial(encode_kernel, chunk), grid=(rows // til...  19.6 us
    all_to_all x1, starting transfers between devices, body(): lax.all_to_all(asked, 'dp', split_axis=0, concat_axis=0, tiled=True)  7.39 us
    all_to_all x1, starting transfers between devices, body(): lax.all_to_all(rows.reshape(n_devices, capacity, width_out), 'dp', split_...  6.01 us
    pallas_call x1, Pallas kernels, gather_rows(): pl.pallas_call(gather_kernel, in_specs=[SMEM, VMEM], out_specs=VMEM, out_...  3.34 us
    unnamed x18, local copies, waits for them, and re-layouts  3.07 us
    pallas_call x1, Pallas kernels, finish(): pl.pallas_call(finish_kernel, in_specs=[SMEM, SMEM, VMEM, VMEM, VMEM], ou...  2.45 us
    pallas_call x1, Pallas kernels, plan(): pl.pallas_call(plan_kernel, in_specs=[VMEM, VMEM], out_specs=[VMEM, VMEM]...  2.12 us
    all_to_all x1, waiting for transfers between devices, body(): lax.all_to_all(rows.reshape(n_devices, capacity, width_out), 'dp', split_...  1.21 us
  transfers between devices with their start and end apart: 2, of which 1 were waited for; matrix products, arithmetic and copies ran while one was open for 4% of the time, Pallas kernels for 41%

profile of v1, /device:TPU:0, one launch (start us, length us, event | category | flops | bytes accessed | tf_op | source)
XLA Modules:
  0.0 47.3 jit_solution(12756768062616121214)
XLA Ops:
  0.0 2.1 %plan.1 = (s32[8,128]{1,0:T(8,128)}, s32[16,128]{1,0:T(8,128)}) custom-call(s32[8,128]{1,0:T(8,128)} %bitcast.14, s32[8,128]{1,0:T(8,128)} %bitcast.15), custom_call_target="tpu_custom_call" | custom-call | tf_op jit(solution)/shard_map/plan/pallas_call | solution.py:59
  2.1 7.4 %all-to-all-start = ((s32[16,1,128]{2,1,0:T(1,128)}), s32[16,1,128]{2,1,0:T(1,128)S(1)}, u32[]{:S(2)}, u32[]{:S(2)}) async-start(s32[16,1,128]{2,1,0:T(1,128)} %bitcast.13), calls=%async_computation | async-start | bytes 16384 | tf_op jit(solution)/shard_map/all_to_all | solution.py:257
  9.5 0.7 %broadcast_in_dim.13.down_bias_ref = f32[1,768]{1,0:T(1,128)S(1)} reshape(f32[768]{0:T(1024)} %param.16) | data formatting | bytes 6144 | tf_op jit(solution)/shard_map/broadcast_in_dim | solution.py:250
  10.2 0.7 %broadcast_in_dim.14.gain_ref = f32[1,768]{1,0:T(1,128)S(1)} reshape(f32[768]{0:T(1024)} %param.17) | data formatting | bytes 6144 | tf_op jit(solution)/shard_map/broadcast_in_dim | solution.py:251
  10.9 0.7 %broadcast_in_dim.15.shift_ref = f32[1,768]{1,0:T(1,128)S(1)} reshape(f32[768]{0:T(1024)} %param.18) | data formatting | bytes 6144 | tf_op jit(solution)/shard_map/broadcast_in_dim | solution.py:251
  11.6 0.0 copy-start
  11.6 1.4 %copy-done = bf16[1024,768]{1,0:T(8,128)(2,1)S(1)} copy-done((bf16[1024,768]{1,0:T(8,128)(2,1)S(1)}, bf16[1024,768]{1,0:T(8,128)(2,1)}, u32[]{:S(2)}) %copy-start) | copy-done | bytes 1572888
  13.0 0.0 copy-start.3
  13.0 0.9 %copy-done.3 = bf16[768,128]{1,0:T(8,128)(2,1)S(1)} copy-done((bf16[768,128]{1,0:T(8,128)(2,1)S(1)}, bf16[768,128]{1,0:T(8,128)(2,1)}, u32[]{:S(2)}) %copy-start.3) | copy-done | bytes 196632
  13.9 0.0 copy-start.5
  13.9 0.7 %copy-done.5 = f32[3072]{0:T(1024)S(1)} copy-done((f32[3072]{0:T(1024)S(1)}, f32[3072]{0:T(1024)}, u32[]{:S(2)}) %copy-start.5) | copy-done | bytes 12312
  14.6 0.0 copy-start.2
  14.6 0.0 copy-start.1
  14.6 0.0 copy-start.4
  14.6 0.0 copy-start.6
  14.6 6.4 %encode.2.first_ref = bf16[256,128]{1,0:T(8,128)(2,1)S(1)} custom-call(bf16[1024,768]{1,0:T(8,128)(2,1)S(1)} %copy-done, bf16[768,3072]{1,0:T(8,128)(2,1)} %up_hbm.3, f32[1,3072]{1,0:T(1,128)S(1)} %bitcast.11, bf16[3072,768]{1,0:T(8,128)(2,1)} %down_hbm.3, f32[1,768]{1,0:T(1,128)S(1)} %broadcast_in_dim.13.down_bias_ref, ...), custom_call_target="tpu_custom_call" | custom-call | flops 2466250752 | bytes 9830400 | tf_op jit(solution)/shard_map/encode/pallas_call | solution.py:211
  21.0 0.0 all-to-all-done
  21.1 0.0 copy-done.2
  21.1 3.3 %gather_rows.1 = bf16[2048,128]{1,0:T(8,128)(2,1)} custom-call(s32[16,128]{1,0:T(8,128)S(1)} %bitcast.10, bf16[4096,128]{1,0:T(8,128)(2,1)S(1)} %copy-done.2), custom_call_target="tpu_custom_call" | custom-call | tf_op jit(solution)/shard_map/gather_rows/pallas_call | solution.py:88
  24.4 6.0 %all-to-all-start.1 = ((bf16[16,128,128]{2,1,0:T(8,128)(2,1)}), bf16[16,128,128]{2,1,0:T(8,128)(2,1)S(1)}, u32[]{:S(2)}, u32[]{:S(2)}) async-start(bf16[16,128,128]{2,1,0:T(8,128)(2,1)} %bitcast.6), calls=%async_computation.1 | async-start | bytes 1048576 | tf_op jit(solution)/shard_map/all_to_all | solution.py:262
  30.4 0.0 copy-done.1
  30.4 0.0 copy-done.4
  30.4 0.0 copy-done.6
  30.5 0.0 copy-start.7
  30.5 0.0 copy-start.8
  30.5 13.2 %encode.3.second_ref = bf16[768,128]{1,0:T(8,128)(2,1)S(1)} custom-call(bf16[1024,768]{1,0:T(8,128)(2,1)S(1)} %copy-done.1, bf16[768,3072]{1,0:T(8,128)(2,1)} %up_hbm.3, f32[1,3072]{1,0:T(1,128)S(1)} %bitcast.12, bf16[3072,768]{1,0:T(8,128)(2,1)} %down_hbm.3, f32[1,768]{1,0:T(1,128)S(1)} %broadcast_in_dim.13.down_bias_ref, ...), custom_call_target="tpu_custom_call" | custom-call | flops 7398752256 | bytes 10616832 | tf_op jit(solution)/shard_map/encode/pallas_call | solution.py:211
  43.7 1.2 %all-to-all-done.1 = bf16[16,128,128]{2,1,0:T(8,128)(2,1)S(1)} async-done(((bf16[16,128,128]{2,1,0:T(8,128)(2,1)}), bf16[16,128,128]{2,1,0:T(8,128)(2,1)S(1)}, u32[]{:S(2)}, u32[]{:S(2)}) %all-to-all-start.1) | async-done | bytes 524320 | tf_op jit(solution)/shard_map/all_to_all | solution.py:262
  44.9 0.0 copy-done.7
  44.9 0.0 copy-done.8
  44.9 2.4 %finish.1 = bf16[1024,128]{1,0:T(8,128)(2,1)} custom-call(s32[8,128]{1,0:T(8,128)S(1)} %copy-done.7, s32[8]{0:T(128)S(1)} %copy-done.8, bf16[256,128]{1,0:T(8,128)(2,1)S(1)} %encode.2.first_ref, bf16[768,128]{1,0:T(8,128)(2,1)S(1)} %encode.3.second_ref, bf16[2048,128]{1,0:T(8,128)(2,1)S(1)} %bitcast.9), custom_call_target="tpu_custom_call" | custom-call | tf_op jit(solution)/shard_map/finish/pallas_call | solution.py:131
Async XLA Ops:
  2.1 18.9 %all-to-all-start = ((s32[16,1,128]{2,1,0:T(1,128)}), s32[16,1,128]{2,1,0:T(1,128)S(1)}, u32[]{:S(2)}, u32[]{:S(2)}) async-start(s32[16,1,128]{2,1,0:T(1,128)} %bitcast.13), calls=%async_computation | async-start | bytes 16384 | tf_op jit(solution)/shard_map/all_to_all | solution.py:257
  11.6 1.4 %copy-start = (bf16[1024,768]{1,0:T(8,128)(2,1)S(1)}, bf16[1024,768]{1,0:T(8,128)(2,1)}, u32[]{:S(2)}) copy-start(bf16[1024,768]{1,0:T(8,128)(2,1)} %rows_ref.2) | copy-start | bytes 4718596
  13.0 0.9 %copy-start.3 = (bf16[768,128]{1,0:T(8,128)(2,1)S(1)}, bf16[768,128]{1,0:T(8,128)(2,1)}, u32[]{:S(2)}) copy-start(bf16[768,128]{1,0:T(8,128)(2,1)} %proj_ref.3) | copy-start | bytes 589828
  13.9 0.7 %copy-start.5 = (f32[3072]{0:T(1024)S(1)}, f32[3072]{0:T(1024)}, u32[]{:S(2)}) copy-start(f32[3072]{0:T(1024)} %param.14) | copy-start | bytes 36868
  14.6 6.4 %copy-start.2 = (bf16[4096,128]{1,0:T(8,128)(2,1)S(1)}, bf16[4096,128]{1,0:T(8,128)(2,1)}, u32[]{:S(2)}) copy-start(bf16[4096,128]{1,0:T(8,128)(2,1)} %table_ref.1) | copy-start | bytes 3145732
  14.6 15.8 %copy-start.1 = (bf16[1024,768]{1,0:T(8,128)(2,1)S(1)}, bf16[1024,768]{1,0:T(8,128)(2,1)}, u32[]{:S(2)}) copy-start(bf16[1024,768]{1,0:T(8,128)(2,1)} %rows_ref.2) | copy-start | bytes 4718596
  14.6 15.8 %copy-start.4 = (bf16[768,128]{1,0:T(8,128)(2,1)S(1)}, bf16[768,128]{1,0:T(8,128)(2,1)}, u32[]{:S(2)}) copy-start(bf16[768,128]{1,0:T(8,128)(2,1)} %proj_ref.3) | copy-start | bytes 589828
  14.6 15.8 %copy-start.6 = (f32[3072]{0:T(1024)S(1)}, f32[3072]{0:T(1024)}, u32[]{:S(2)}) copy-start(f32[3072]{0:T(1024)} %param.14) | copy-start | bytes 36868
  24.4 20.5 %all-to-all-start.1 = ((bf16[16,128,128]{2,1,0:T(8,128)(2,1)}), bf16[16,128,128]{2,1,0:T(8,128)(2,1)S(1)}, u32[]{:S(2)}, u32[]{:S(2)}) async-start(bf16[16,128,128]{2,1,0:T(8,128)(2,1)} %bitcast.6), calls=%async_computation.1 | async-start | bytes 1048576 | tf_op jit(solution)/shard_map/all_to_all | solution.py:262
  30.5 14.4 %copy-start.7 = (s32[8,128]{1,0:T(8,128)S(1)}, s32[8,128]{1,0:T(8,128)}, u32[]{:S(2)}) copy-start(s32[8,128]{1,0:T(8,128)} %get-tuple-element.13.slots_ref) | copy-start | bytes 12292
  30.5 14.4 %copy-start.8 = (s32[8]{0:T(128)S(1)}, s32[8]{0:T(128)}, u32[]{:S(2)}) copy-start(s32[8]{0:T(128)} %lengths_ref.1) | copy-start | bytes 100

commit v2 on v1

v2 whole, which is shorter than its diff:
```python
import functools

import jax
import jax.numpy as jnp
from jax import lax
from jax.experimental import pallas as pl
from jax.experimental.pallas import tpu as pltpu
from jax.sharding import PartitionSpec as P

LEN = 128
LANES = 128
LOW = 64
COUNT = 65536
GROUP = 16
AHEAD = 2
VMEM_BYTES = 60 * 2**20
VMEM = pl.BlockSpec(memory_space=pltpu.VMEM)
SMEM = pl.BlockSpec(memory_space=pltpu.SMEM)
HBM = pl.BlockSpec(memory_space=pltpu.HBM)


def plan_kernel(lengths_ref, owners_ref, ids_ref, slots_ref, asked_ref):
    n_owners, capacity = asked_ref.shape
    n_rows = owners_ref.shape[0]
    owner_iota = lax.broadcasted_iota(jnp.int32, (n_owners, LANES), 0)
    slot_iota = lax.broadcasted_iota(jnp.int32, (capacity, LANES), 0)
    lane = lax.broadcasted_iota(jnp.int32, (1, LANES), 1)
    before = lax.broadcasted_iota(jnp.int32, (LANES, LANES), 0) < lax.broadcasted_iota(
        jnp.int32, (LANES, LANES), 1
    )
    counter = jnp.concatenate(
        [before.astype(jnp.float32), jnp.ones((LANES, LANES), jnp.float32)], axis=1
    ).astype(jnp.bfloat16)
    owner_rows = [owners_ref[row : row + 1, :] for row in range(n_rows)]
    live = [lane < lengths_ref[row] for row in range(n_rows)]
    hot = [
        ((owner_iota == owner_rows[row]) & live[row]).astype(jnp.float32) for row in range(n_rows)
    ]
    counts = jnp.dot(
        jnp.concatenate(hot, axis=0).astype(jnp.bfloat16),
        counter,
        preferred_element_type=jnp.float32,
    )
    named = jnp.zeros((n_owners, LANES), jnp.float32)
    placed, parts = [], []
    for row in range(n_rows):
        mine = counts[row * n_owners : (row + 1) * n_owners]
        slot = jnp.sum(hot[row] * (mine[:, :LANES] + named), axis=0, keepdims=True).astype(
            jnp.int32
        )
        named = named + mine[:, LANES:]
        slots_ref[row : row + 1, :] = jnp.where(live[row], owner_rows[row] * capacity + slot, 0)
        placed.append((slot_iota == slot).astype(jnp.float32).astype(jnp.bfloat16))
        ids_row = ids_ref[row : row + 1, :]
        parts.append(
            jnp.concatenate(
                [
                    hot[row] * (ids_row // LOW).astype(jnp.float32),
                    hot[row] * (ids_row % LOW).astype(jnp.float32),
                ],
                axis=0,
            ).astype(jnp.bfloat16)
        )
    both = lax.dot_general(
        jnp.concatenate(parts, axis=1),
        jnp.concatenate(placed, axis=1),
        (((1,), (1,)), ((), ())),
        preferred_element_type=jnp.float32,
    )
    ids = both[:n_owners].astype(jnp.int32) * LOW + both[n_owners:].astype(jnp.int32)
    first = lax.broadcasted_iota(jnp.int32, (n_owners, capacity), 1) == 0
    asked_ref[...] = ids + jnp.where(first, named[:, :capacity].astype(jnp.int32) * COUNT, 0)


def plan(lengths, owners, local_ids, n_owners, capacity):
    rows = owners.shape[0]
    return pl.pallas_call(
        plan_kernel,
        in_specs=[SMEM, VMEM, VMEM],
        out_specs=[VMEM, VMEM],
        out_shape=[
            jax.ShapeDtypeStruct((rows, LANES), jnp.int32),
            jax.ShapeDtypeStruct((n_owners, capacity), jnp.int32),
        ],
        name="plan",
    )(lengths, owners, local_ids)


def gather_kernel(asked_ref, table_ref, out_ref, table_f32, out_f32):
    n_owners, capacity = asked_ref.shape
    table_f32[...] = table_ref[...].astype(jnp.float32)

    def device(source, carry):
        groups = (asked_ref[source, 0] // COUNT + GROUP - 1) // GROUP

        def group(index, carry):
            start = index * GROUP
            for slot in range(GROUP):
                row = asked_ref[source, start + slot] % COUNT
                out_f32[pl.ds(source * capacity + start + slot, 1), :] = table_f32[
                    pl.ds(row, 1), :
                ]
            return carry

        return lax.fori_loop(0, groups, group, carry)

    lax.fori_loop(0, n_owners, device, 0)
    out_ref[...] = out_f32[...].astype(jnp.bfloat16)


def gather_rows(asked, table):
    rows = asked.shape[0] * asked.shape[1]
    width = table.shape[1]
    return pl.pallas_call(
        gather_kernel,
        in_specs=[SMEM, VMEM],
        out_specs=VMEM,
        out_shape=jax.ShapeDtypeStruct((rows, width), jnp.bfloat16),
        scratch_shapes=[
            pltpu.VMEM(table.shape, jnp.float32),
            pltpu.VMEM((rows, width), jnp.float32),
        ],
        compiler_params=pltpu.CompilerParams(vmem_limit_bytes=16 * 2**20),
        name="gather_rows",
    )(asked, table)


def finish_kernel(slots_ref, lengths_ref, first_ref, second_ref, centers_ref, out_ref, centers_f32, mine):
    centers_f32[...] = centers_ref[...].astype(jnp.float32)
    n_passages = out_ref.shape[0] // LEN
    split = first_ref.shape[0] // LEN

    def passage_rows(passage, carry):
        groups = (lengths_ref[passage] + GROUP - 1) // GROUP

        def group(index, carry):
            start = index * GROUP
            for position in range(GROUP):
                row = slots_ref[passage, start + position]
                mine[pl.ds(passage * LEN + start + position, 1), :] = centers_f32[
                    pl.ds(row, 1), :
                ]
            return carry

        return lax.fori_loop(0, groups, group, carry)

    lax.fori_loop(0, n_passages, passage_rows, 0)
    position = lax.broadcasted_iota(jnp.int32, (LEN, 1), 0)
    for passage in range(n_passages):
        at = slice(passage * LEN, (passage + 1) * LEN)
        if passage < split:
            embedded = first_ref[at, :]
        else:
            embedded = second_ref[(passage - split) * LEN : (passage - split + 1) * LEN, :]
        difference = embedded.astype(jnp.float32) - mine[at, :]
        total = jnp.sum(difference * difference, axis=1, keepdims=True)
        result = difference * lax.rsqrt(total + 1e-06)
        alive = position < lengths_ref[passage]
        out_ref[at, :] = jnp.where(alive, result, 0.0).astype(jnp.bfloat16)


def finish(slots, lengths, first, second, centers):
    rows = slots.shape[0] * slots.shape[1]
    width = centers.shape[1]
    return pl.pallas_call(
        finish_kernel,
        in_specs=[SMEM, SMEM, VMEM, VMEM, VMEM],
        out_specs=VMEM,
        out_shape=jax.ShapeDtypeStruct((rows, width), jnp.bfloat16),
        scratch_shapes=[
            pltpu.VMEM(centers.shape, jnp.float32),
            pltpu.VMEM((rows, width), jnp.float32),
        ],
        compiler_params=pltpu.CompilerParams(vmem_limit_bytes=16 * 2**20),
        name="finish",
    )(slots, lengths, first, second, centers)


def encode_kernel(
    start, chunk, rows_hbm, up_hbm, up_bias_hbm, down_hbm, down_bias_hbm, gain_hbm, shift_hbm, proj_hbm,
    out_ref, rows_vmem, up_vmem, up_bias, down_vmem, down_bias, gain, shift, proj,
    rows_in, weights_in, small_in,
):
    n_chunks = up_vmem.shape[0]
    tile_rows = rows_vmem.shape[1]
    tile_index = pl.program_id(0)

    def rows_copy(index):
        return pltpu.make_async_copy(
            rows_hbm.at[pl.ds(start + index * tile_rows, tile_rows), :],
            rows_vmem.at[index],
            rows_in.at[index],
        )

    def up_copy(index):
        return pltpu.make_async_copy(
            up_hbm.at[:, pl.ds(index * chunk, chunk)], up_vmem.at[index], weights_in.at[0, index]
        )

    def down_copy(index):
        return pltpu.make_async_copy(
            down_hbm.at[pl.ds(index * chunk, chunk), :], down_vmem.at[index], weights_in.at[1, index]
        )

    up_bias_copy = pltpu.make_async_copy(up_bias_hbm, up_bias, small_in.at[0])
    last_copies = [
        pltpu.make_async_copy(source, target, small_in.at[1 + index])
        for index, (source, target) in enumerate(
            [
                (down_bias_hbm, down_bias),
                (gain_hbm, gain),
                (shift_hbm, shift),
                (proj_hbm, proj),
            ]
        )
    ]

    queue = [down_copy(0)]
    for index in range(1, n_chunks):
        queue += [up_copy(index), down_copy(index)]
    queue += last_copies + [rows_copy(index) for index in range(1, rows_vmem.shape[0])]

    def start_next(done):
        for copy in queue[AHEAD + done : AHEAD + done + 1]:
            copy.start()

    def tile(first):
        rows = rows_vmem[tile_index]
        total = None
        for index in range(n_chunks):
            if first:
                up_copy(index).wait()
                start_next(2 * index)
            up_proj = (
                jnp.dot(rows, up_vmem[index], preferred_element_type=jnp.float32)
                + up_bias[index * chunk : (index + 1) * chunk][None, :]
            )
            activated = (0.5 * up_proj * (1.0 + lax.erf(up_proj * 0.7071067811865476))).astype(
                jnp.bfloat16
            )
            if first:
                down_copy(index).wait()
                start_next(2 * index + 1)
            part = jnp.dot(activated, down_vmem[index], preferred_element_type=jnp.float32)
            total = part if total is None else total + part
        if first:
            for copy in queue[AHEAD + 2 * n_chunks :]:
                copy.start()
            for copy in last_copies:
                copy.wait()
        ffn_out = total + down_bias[...][None, :] + rows.astype(jnp.float32)
        center = jnp.mean(ffn_out, axis=1, keepdims=True)
        centered = ffn_out - center
        spread = jnp.mean(centered * centered, axis=1, keepdims=True)
        normed = (
            centered * lax.rsqrt(spread + 1e-05) * gain[...][None, :] + shift[...][None, :]
        ).astype(jnp.bfloat16)
        projected = jnp.dot(normed, proj[...], preferred_element_type=jnp.float32)
        size = jnp.sum(projected * projected, axis=1, keepdims=True)
        out_ref[...] = (projected * lax.rsqrt(size + 1e-06)).astype(jnp.bfloat16)

    @pl.when(tile_index == 0)
    def _():
        rows_copy(0).start()
        up_copy(0).start()
        up_bias_copy.start()
        for copy in queue[:AHEAD]:
            copy.start()
        up_bias_copy.wait()
        rows_copy(0).wait()
        tile(True)

    @pl.when(tile_index > 0)
    def _():
        rows_copy(tile_index).wait()
        tile(False)


def encode(hidden_in, weights, start, rows, tile_rows, chunk):
    up_weight, up_bias, down_weight, down_bias, norm_gain, norm_shift, proj_weight = weights
    width, hidden = up_weight.shape
    out_width = proj_weight.shape[1]
    n_chunks = hidden // chunk
    n_tiles = rows // tile_rows
    return pl.pallas_call(
        functools.partial(encode_kernel, start, chunk),
        grid=(n_tiles,),
        in_specs=[HBM] * 8,
        out_specs=pl.BlockSpec((tile_rows, out_width), lambda index: (index, 0)),
        out_shape=jax.ShapeDtypeStruct((rows, out_width), jnp.bfloat16),
        scratch_shapes=[
            pltpu.VMEM((n_tiles, tile_rows, width), jnp.bfloat16),
            pltpu.VMEM((n_chunks, width, chunk), jnp.bfloat16),
            pltpu.VMEM(up_bias.shape, jnp.float32),
            pltpu.VMEM((n_chunks, chunk, width), jnp.bfloat16),
            pltpu.VMEM(down_bias.shape, jnp.float32),
            pltpu.VMEM(norm_gain.shape, jnp.float32),
            pltpu.VMEM(norm_shift.shape, jnp.float32),
            pltpu.VMEM(proj_weight.shape, jnp.bfloat16),
            pltpu.SemaphoreType.DMA((n_tiles,)),
            pltpu.SemaphoreType.DMA((2, n_chunks)),
            pltpu.SemaphoreType.DMA((5,)),
        ],
        compiler_params=pltpu.CompilerParams(vmem_limit_bytes=VMEM_BYTES),
        cost_estimate=pl.CostEstimate(
            flops=2 * rows * (2 * width * hidden + width * out_width),
            bytes_accessed=4 * width * hidden + 2 * rows * width,
            transcendentals=0,
        ),
        name="encode",
    )(hidden_in, up_weight, up_bias, down_weight, down_bias, norm_gain, norm_shift, proj_weight)


def body(
    hidden_in, up_weight, up_bias, down_weight, down_bias, norm_gain, norm_shift, proj_weight,
    centroids, lengths, owners, local_ids,
):
    n_devices = lax.axis_size("dp")
    token_rows = hidden_in.shape[0]
    width_out = proj_weight.shape[1]
    capacity = max(2, 2 * token_rows // n_devices)
    weights = (
        up_weight, up_bias, down_weight, down_bias, norm_gain, norm_shift, proj_weight,
    )
    early = token_rows // 4
    slots, asked = plan(
        lengths, owners.reshape(-1, LANES), local_ids.reshape(-1, LANES), n_devices, capacity
    )
    arrived = lax.all_to_all(asked, "dp", split_axis=0, concat_axis=0, tiled=True)
    first = encode(hidden_in, weights, 0, early, 256, 768)
    arrived, first = lax.optimization_barrier((arrived, first))
    rows = gather_rows(arrived, centroids)
    hidden_in, rows = lax.optimization_barrier((hidden_in, rows))
    centers = lax.all_to_all(
        rows.reshape(n_devices, capacity, width_out), "dp", split_axis=0, concat_axis=0, tiled=True
    )
    second = encode(hidden_in, weights, early, token_rows - early, 384, 768)
    centers, second = lax.optimization_barrier((centers, second))
    return finish(slots, lengths, first, second, centers.reshape(-1, width_out))


def solution(mesh):
    in_specs = (
        P(("groups", "dp"), None),
        P(),
        P(),
        P(),
        P(),
        P(),
        P(),
        P(),
        P("dp", None),
        P(("groups", "dp")),
        P(("groups", "dp"), None),
        P(("groups", "dp")),
    )
    out_specs = P(("groups", "dp"), None)
    return jax.shard_map(body, mesh=mesh, in_specs=in_specs, out_specs=out_specs, check_vma=False)
```

time: 47.8 us -> 52.6 us (1.10)
  Pallas kernels: 27.5 us -> 34.7 us
  local copies, waits for them, and re-layouts: 5.14 us -> 0.94 us
  starting transfers between devices: 13.4 us -> 16.4 us
  waiting for transfers between devices: 1.21 us -> 0.01 us
    pallas_call x1, Pallas kernels: 3.34 us -> 7.18 us  [gather_rows(): pl.pallas_call(gather_kernel, in_specs=[SMEM, VMEM], out_specs=VMEM, out_...]
    all_to_all x1, starting transfers between devices: 6.01 us -> 9.05 us  [body(): lax.all_to_all(rows.reshape(n_devices, capacity, width_out), 'dp', split_...]
    pallas_call x3, Pallas kernels: 21.7 us -> 24.2 us  [the longest x2 22.5 us: encode(): pl.pallas_call(functools.partial(encode_kernel, start, chunk), grid=(n_ti...]
    unnamed x18 -> x10, local copies, waits for them, and re-layouts: 3.07 us -> 0.94 us
    broadcast_in_dim x3 -> x0, local copies, waits for them, and re-layouts: 2.07 us -> none  [the longest x1 0.69 us: body(): down_bias[None, :]]
    all_to_all x1, waiting for transfers between devices: 1.21 us -> 0.01 us  [body(): lax.all_to_all(rows.reshape(n_devices, capacity, width_out), 'dp', split_...]
    pallas_call x1, Pallas kernels: 2.45 us -> 3.38 us  [finish(): pl.pallas_call(finish_kernel, in_specs=[SMEM, SMEM, VMEM, VMEM, VMEM], ou...]
  transfers between devices with their start and end apart: 2 -> 2, of which waited for: 1 -> 0; matrix products, arithmetic and copies ran while one was open for 4% -> 0% of each run, Pallas kernels for 41% -> 43%
where the time goes in v2:
time: 52.6 us; the launch traced here: 52.3 us
  Pallas kernels  34.7 us (66%)
  starting transfers between devices  16.4 us (31%)
  local copies, waits for them, and re-layouts  0.94 us (2%)
    pallas_call x2, Pallas kernels, encode(): pl.pallas_call(functools.partial(encode_kernel, start, chunk), grid=(n_ti...  22.5 us
    all_to_all x1, starting transfers between devices, body(): lax.all_to_all(rows.reshape(n_devices, capacity, width_out), 'dp', split_...  9.05 us
    all_to_all x1, starting transfers between devices, body(): lax.all_to_all(asked, 'dp', split_axis=0, concat_axis=0, tiled=True)  7.39 us
    pallas_call x1, Pallas kernels, gather_rows(): pl.pallas_call(gather_kernel, in_specs=[SMEM, VMEM], out_specs=VMEM, out_...  7.18 us
    pallas_call x1, Pallas kernels, finish(): pl.pallas_call(finish_kernel, in_specs=[SMEM, SMEM, VMEM, VMEM, VMEM], ou...  3.38 us
    pallas_call x1, Pallas kernels, plan(): pl.pallas_call(plan_kernel, in_specs=[SMEM, VMEM, VMEM], out_specs=[VMEM,...  1.68 us
  transfers between devices with their start and end apart: 2, of which 0 were waited for; matrix products, arithmetic and copies ran while one was open for 0% of the time, Pallas kernels for 43%

profile of v2, /device:TPU:0, one launch (start us, length us, event | category | flops | bytes accessed | tf_op | source)
XLA Modules:
  0.0 52.3 jit_solution(10232949495408372778)
XLA Ops:
  0.0 1.7 %plan.1 = (s32[8,128]{1,0:T(8,128)}, s32[16,128]{1,0:T(8,128)}) custom-call(s32[8]{0:T(128)} %lengths_ref.3, s32[8,128]{1,0:T(8,128)} %bitcast.11, s32[8,128]{1,0:T(8,128)} %bitcast.12), custom_call_target="tpu_custom_call" | custom-call | tf_op jit(solution)/shard_map/plan/pallas_call | solution.py:77
  1.7 7.4 %all-to-all-start = ((s32[16,1,128]{2,1,0:T(1,128)}), s32[16,1,128]{2,1,0:T(1,128)S(1)}, u32[]{:S(2)}, u32[]{:S(2)}) async-start(s32[16,1,128]{2,1,0:T(1,128)} %bitcast.10), calls=%async_computation | async-start | bytes 16384 | tf_op jit(solution)/shard_map/all_to_all | solution.py:329
  9.1 0.0 copy-start
  9.1 8.0 %encode.2.first_ref = bf16[256,128]{1,0:T(8,128)(2,1)} custom-call(bf16[1024,768]{1,0:T(8,128)(2,1)} %rows_hbm.2, bf16[768,3072]{1,0:T(8,128)(2,1)} %up_hbm.3, f32[3072]{0:T(1024)} %up_bias_hbm.3, bf16[3072,768]{1,0:T(8,128)(2,1)} %down_hbm.3, f32[768]{0:T(1024)} %down_bias_hbm.3, f32[768]{0:T(1024)} %gain_hbm.3, f32[768]{0:T(1024)} %shift_hbm.3, ...), custom_call_target="tpu_custom_call" | custom-call | flops 2466250752 | bytes 9830400 | tf_op jit(solution)/shard_map/encode/pallas_call | solution.py:285
  17.1 0.0 all-to-all-done
  17.1 0.0 copy-done
  17.1 7.2 %gather_rows.1 = bf16[2048,128]{1,0:T(8,128)(2,1)} custom-call(s32[16,128]{1,0:T(8,128)S(1)} %bitcast.9, bf16[4096,128]{1,0:T(8,128)(2,1)S(1)} %copy-done), custom_call_target="tpu_custom_call" | custom-call | tf_op jit(solution)/shard_map/gather_rows/pallas_call | solution.py:114
  24.3 9.1 %all-to-all-start.1 = ((bf16[16,128,128]{2,1,0:T(8,128)(2,1)}), bf16[16,128,128]{2,1,0:T(8,128)(2,1)S(1)}, u32[]{:S(2)}, u32[]{:S(2)}) async-start(bf16[16,128,128]{2,1,0:T(8,128)(2,1)} %bitcast.5), calls=%async_computation.1 | async-start | bytes 1048576 | tf_op jit(solution)/shard_map/all_to_all | solution.py:334
  33.4 0.0 copy-start.1
  33.4 0.0 copy-start.3
  33.4 0.0 copy-start.4
  33.4 14.5 %encode.3.second_ref = bf16[768,128]{1,0:T(8,128)(2,1)} custom-call(bf16[1024,768]{1,0:T(8,128)(2,1)} %rows_hbm.2, bf16[768,3072]{1,0:T(8,128)(2,1)} %up_hbm.3, f32[3072]{0:T(1024)} %up_bias_hbm.3, bf16[3072,768]{1,0:T(8,128)(2,1)} %down_hbm.3, f32[768]{0:T(1024)} %down_bias_hbm.3, f32[768]{0:T(1024)} %gain_hbm.3, f32[768]{0:T(1024)} %shift_hbm.3, ...), custom_call_target="tpu_custom_call" | custom-call | flops 7398752256 | bytes 10616832 | tf_op jit(solution)/shard_map/encode/pallas_call | solution.py:285
  47.9 0.0 all-to-all-done.1
  47.9 0.0 copy-done.1
  47.9 0.0 copy-done.3
  47.9 0.0 copy-done.4
  47.9 0.0 copy-start.2
  48.0 0.9 %copy-done.2 = bf16[768,128]{1,0:T(8,128)(2,1)S(1)} copy-done((bf16[768,128]{1,0:T(8,128)(2,1)S(1)}, bf16[768,128]{1,0:T(8,128)(2,1)}, u32[]{:S(2)}) %copy-start.2) | copy-done | bytes 196632
  48.9 3.4 %finish.1 = bf16[1024,128]{1,0:T(8,128)(2,1)} custom-call(s32[8,128]{1,0:T(8,128)S(1)} %copy-done.3, s32[8]{0:T(128)S(1)} %copy-done.4, bf16[256,128]{1,0:T(8,128)(2,1)S(1)} %copy-done.1, bf16[768,128]{1,0:T(8,128)(2,1)S(1)} %copy-done.2, bf16[2048,128]{1,0:T(8,128)(2,1)S(1)} %bitcast.8), custom_call_target="tpu_custom_call" | custom-call | tf_op jit(solution)/shard_map/finish/pallas_call | solution.py:165
Async XLA Ops:
  1.7 15.4 %all-to-all-start = ((s32[16,1,128]{2,1,0:T(1,128)}), s32[16,1,128]{2,1,0:T(1,128)S(1)}, u32[]{:S(2)}, u32[]{:S(2)}) async-start(s32[16,1,128]{2,1,0:T(1,128)} %bitcast.10), calls=%async_computation | async-start | bytes 16384 | tf_op jit(solution)/shard_map/all_to_all | solution.py:329
  9.1 8.0 %copy-start = (bf16[4096,128]{1,0:T(8,128)(2,1)S(1)}, bf16[4096,128]{1,0:T(8,128)(2,1)}, u32[]{:S(2)}) copy-start(bf16[4096,128]{1,0:T(8,128)(2,1)} %table_ref.1) | copy-start | bytes 3145732
  24.3 23.6 %all-to-all-start.1 = ((bf16[16,128,128]{2,1,0:T(8,128)(2,1)}), bf16[16,128,128]{2,1,0:T(8,128)(2,1)S(1)}, u32[]{:S(2)}, u32[]{:S(2)}) async-start(bf16[16,128,128]{2,1,0:T(8,128)(2,1)} %bitcast.5), calls=%async_computation.1 | async-start | bytes 1048576 | tf_op jit(solution)/shard_map/all_to_all | solution.py:334
  33.4 14.6 %copy-start.1 = (bf16[256,128]{1,0:T(8,128)(2,1)S(1)}, bf16[256,128]{1,0:T(8,128)(2,1)}, u32[]{:S(2)}) copy-start(bf16[256,128]{1,0:T(8,128)(2,1)} %encode.2.first_ref) | copy-start | bytes 196612
  33.4 14.6 %copy-start.3 = (s32[8,128]{1,0:T(8,128)S(1)}, s32[8,128]{1,0:T(8,128)}, u32[]{:S(2)}) copy-start(s32[8,128]{1,0:T(8,128)} %get-tuple-element.13.slots_ref) | copy-start | bytes 12292
  33.4 14.6 %copy-start.4 = (s32[8]{0:T(128)S(1)}, s32[8]{0:T(128)}, u32[]{:S(2)}) copy-start(s32[8]{0:T(128)} %lengths_ref.3) | copy-start | bytes 100
  47.9 0.9 %copy-start.2 = (bf16[768,128]{1,0:T(8,128)(2,1)S(1)}, bf16[768,128]{1,0:T(8,128)(2,1)}, u32[]{:S(2)}) copy-start(bf16[768,128]{1,0:T(8,128)(2,1)} %encode.3.second_ref) | copy-start | bytes 589828

commit v3 on v2

v3 whole, which is shorter than its diff:
```python
import functools

import jax
import jax.numpy as jnp
from jax import lax
from jax.experimental import pallas as pl
from jax.experimental.pallas import tpu as pltpu
from jax.sharding import PartitionSpec as P

LEN = 128
LANES = 128
LOW_BITS = 6
LOW = 1 << LOW_BITS
COUNT_SHIFT = 16
BLOCK = 32
VMEM_BYTES = 16 * 2**20
ENC_BYTES = 48 * 2**20
AHEAD = 3
VMEM = pl.BlockSpec(memory_space=pltpu.VMEM)
SMEM = pl.BlockSpec(memory_space=pltpu.SMEM)
HBM = pl.BlockSpec(memory_space=pltpu.HBM)


def plan_kernel(lengths_ref, owners_ref, ids_ref, slots_ref, asked_ref):
    n_owners, capacity = asked_ref.shape
    n_rows = owners_ref.shape[0]
    owner_iota = lax.broadcasted_iota(jnp.int32, (n_owners, LANES), 0)
    slot_iota = lax.broadcasted_iota(jnp.int32, (capacity, LANES), 0)
    lane = lax.broadcasted_iota(jnp.int32, (1, LANES), 1)
    before = lax.broadcasted_iota(jnp.int32, (LANES, LANES), 0) < lax.broadcasted_iota(
        jnp.int32, (LANES, LANES), 1
    )
    counter = jnp.concatenate(
        [before.astype(jnp.float32), jnp.ones((LANES, LANES), jnp.float32)], axis=1
    ).astype(jnp.bfloat16)
    owner_rows = [owners_ref[row : row + 1, :] for row in range(n_rows)]
    live = [lane < lengths_ref[row] for row in range(n_rows)]
    hot = [
        ((owner_iota == owner_rows[row]) & live[row]).astype(jnp.float32) for row in range(n_rows)
    ]
    counts = jnp.dot(
        jnp.concatenate(hot, axis=0).astype(jnp.bfloat16),
        counter,
        preferred_element_type=jnp.float32,
    )
    named = jnp.zeros((n_owners, LANES), jnp.float32)
    placed, parts = [], []
    for row in range(n_rows):
        mine = counts[row * n_owners : (row + 1) * n_owners]
        slot = jnp.sum(hot[row] * (mine[:, :LANES] + named), axis=0, keepdims=True).astype(
            jnp.int32
        )
        named = named + mine[:, LANES:]
        slots_ref[n_rows + row : n_rows + row + 1, :] = jnp.full(
            (1, LANES), lengths_ref[row], jnp.int32
        )
        slots_ref[row : row + 1, :] = jnp.where(live[row], owner_rows[row] * capacity + slot, 0)
        placed.append((slot_iota == slot).astype(jnp.float32).astype(jnp.bfloat16))
        ids_row = ids_ref[row : row + 1, :]
        parts.append(
            jnp.concatenate(
                [
                    hot[row] * ((ids_row >> LOW_BITS)).astype(jnp.float32),
                    hot[row] * ((ids_row & (LOW - 1))).astype(jnp.float32),
                ],
                axis=0,
            ).astype(jnp.bfloat16)
        )
    both = lax.dot_general(
        jnp.concatenate(parts, axis=1),
        jnp.concatenate(placed, axis=1),
        (((1,), (1,)), ((), ())),
        preferred_element_type=jnp.float32,
    )
    ids = both[:n_owners].astype(jnp.int32) * LOW + both[n_owners:].astype(jnp.int32)
    first = lax.broadcasted_iota(jnp.int32, (n_owners, capacity), 1) == 0
    asked_ref[...] = ids + jnp.where(first, named[:, :capacity].astype(jnp.int32) << COUNT_SHIFT, 0)


def plan(lengths, owners, local_ids, n_owners, capacity):
    rows = owners.shape[0]
    return pl.pallas_call(
        plan_kernel,
        in_specs=[SMEM, VMEM, VMEM],
        out_specs=[VMEM, VMEM],
        out_shape=[
            jax.ShapeDtypeStruct((2 * rows, LANES), jnp.int32),
            jax.ShapeDtypeStruct((n_owners, capacity), jnp.int32),
        ],
        cost_estimate=pl.CostEstimate(flops=2 * 10**10, bytes_accessed=2**20, transcendentals=0),
        name="plan",
    )(lengths, owners, local_ids)


def gather_kernel(asked_ref, table_ref, out_ref, table_f32, out_f32):
    n_owners, capacity = asked_ref.shape
    table_f32[...] = table_ref[...].astype(jnp.float32)

    block = min(BLOCK, capacity)

    def device(source, carry):
        count = asked_ref[source, 0] >> COUNT_SHIFT
        base = source * capacity
        for start in range(0, capacity, block):

            @pl.when(count > start)
            def _():
                for slot in range(start, start + block):
                    row = asked_ref[source, slot]
                    if slot == 0:
                        row = row & ((1 << COUNT_SHIFT) - 1)
                    out_f32[pl.ds(base + slot, 1), :] = table_f32[pl.ds(row, 1), :]

        return carry

    lax.fori_loop(0, n_owners, device, 0)
    out_ref[...] = out_f32[...].astype(jnp.bfloat16)


def gather_rows(asked, table):
    rows = asked.shape[0] * asked.shape[1]
    width = table.shape[1]
    return pl.pallas_call(
        gather_kernel,
        in_specs=[SMEM, VMEM],
        out_specs=VMEM,
        out_shape=jax.ShapeDtypeStruct((rows, width), jnp.bfloat16),
        scratch_shapes=[
            pltpu.VMEM(table.shape, jnp.float32),
            pltpu.VMEM((rows, width), jnp.float32),
        ],
        compiler_params=pltpu.CompilerParams(vmem_limit_bytes=VMEM_BYTES),
        cost_estimate=pl.CostEstimate(flops=2 * 10**10, bytes_accessed=2**20, transcendentals=0),
        name="gather_rows",
    )(asked, table)


def finish_kernel(slots_ref, embedded_ref, centers_ref, out_ref, centers_f32, mine):
    centers_f32[...] = centers_ref[...].astype(jnp.float32)
    n_passages = out_ref.shape[0] // LEN

    def passage_rows(passage, carry):
        length = slots_ref[n_passages + passage, 0]
        base = passage * LEN
        for start in range(0, LEN, BLOCK):

            @pl.when(length > start)
            def _():
                for position in range(start, start + BLOCK):
                    row = slots_ref[passage, position]
                    mine[pl.ds(base + position, 1), :] = centers_f32[pl.ds(row, 1), :]

        return carry

    lax.fori_loop(0, n_passages, passage_rows, 0)
    position = lax.broadcasted_iota(jnp.int32, (LEN, 1), 0)
    for passage in range(n_passages):
        at = slice(passage * LEN, (passage + 1) * LEN)
        difference = embedded_ref[at, :].astype(jnp.float32) - mine[at, :]
        total = jnp.sum(difference * difference, axis=1, keepdims=True)
        result = difference * lax.rsqrt(total + 1e-06)
        alive = position < slots_ref[n_passages + passage, 0]
        out_ref[at, :] = jnp.where(alive, result, 0.0).astype(jnp.bfloat16)


def finish(slots, embedded, centers):
    rows = embedded.shape[0]
    width = centers.shape[1]
    return pl.pallas_call(
        finish_kernel,
        in_specs=[SMEM, VMEM, VMEM],
        out_specs=VMEM,
        out_shape=jax.ShapeDtypeStruct((rows, width), jnp.bfloat16),
        scratch_shapes=[
            pltpu.VMEM(centers.shape, jnp.float32),
            pltpu.VMEM((rows, width), jnp.float32),
        ],
        compiler_params=pltpu.CompilerParams(vmem_limit_bytes=VMEM_BYTES),
        name="finish",
    )(slots, embedded, centers)


def encode_kernel(
    tile_rows, chunk, rows_ref, up_hbm, up_bias, down_hbm, down_bias, gain, shift, proj, out_ref,
    up_vmem, down_vmem, arrived,
):
    n_chunks = up_vmem.shape[0]
    queue = []
    for index in range(n_chunks):
        at = pl.ds(index * chunk, chunk)
        queue += [
            pltpu.make_async_copy(up_hbm.at[:, at], up_vmem.at[index], arrived.at[2 * index]),
            pltpu.make_async_copy(
                down_hbm.at[at, :], down_vmem.at[index], arrived.at[2 * index + 1]
            ),
        ]

    def wait_weights(index):
        queue[index].wait()
        for copy in queue[index + AHEAD : index + AHEAD + 1]:
            copy.start()

    def tile(start, first):
        at = pl.ds(start, tile_rows)
        rows = rows_ref[at, :]

        def up(index):
            return (
                jnp.dot(rows, up_vmem[index], preferred_element_type=jnp.float32)
                + up_bias[index * chunk : (index + 1) * chunk][None, :]
            )

        total = None
        if first:
            wait_weights(0)
        up_proj = up(0)
        for index in range(n_chunks):
            if first:
                wait_weights(2 * index + 1)
                if index + 1 < n_chunks:
                    wait_weights(2 * index + 2)
            following = up(index + 1) if first and index + 1 < n_chunks else None
            if not first and index > 0:
                up_proj = up(index)
            activated = (0.5 * up_proj * (1.0 + lax.erf(up_proj * 0.7071067811865476))).astype(
                jnp.bfloat16
            )
            part = jnp.dot(activated, down_vmem[index], preferred_element_type=jnp.float32)
            total = part if total is None else total + part
            up_proj = following
        ffn_out = total + down_bias[...][None, :] + rows.astype(jnp.float32)
        center = jnp.mean(ffn_out, axis=1, keepdims=True)
        centered = ffn_out - center
        spread = jnp.mean(centered * centered, axis=1, keepdims=True)
        normed = (
            centered * lax.rsqrt(spread + 1e-05) * gain[...][None, :] + shift[...][None, :]
        ).astype(jnp.bfloat16)
        projected = jnp.dot(normed, proj[...], preferred_element_type=jnp.float32)
        size = jnp.sum(projected * projected, axis=1, keepdims=True)
        out_ref[at, :] = (projected * lax.rsqrt(size + 1e-06)).astype(jnp.bfloat16)

    for copy in queue[:AHEAD]:
        copy.start()
    tile(0, True)

    def later(index, carry):
        tile(pl.multiple_of(index * tile_rows, tile_rows), False)
        return carry

    lax.fori_loop(1, out_ref.shape[0] // tile_rows, later, 0)


def encode(hidden_in, weights, start, rows, tile_rows, chunk):
    up_weight, up_bias, down_weight, down_bias, norm_gain, norm_shift, proj_weight = weights
    width, hidden = up_weight.shape
    out_width = proj_weight.shape[1]
    n_chunks = hidden // chunk
    return pl.pallas_call(
        functools.partial(encode_kernel, tile_rows, chunk),
        in_specs=[VMEM, HBM, VMEM, HBM, VMEM, VMEM, VMEM, VMEM],
        out_specs=VMEM,
        out_shape=jax.ShapeDtypeStruct((rows, out_width), jnp.bfloat16),
        scratch_shapes=[
            pltpu.VMEM((n_chunks, width, chunk), jnp.bfloat16),
            pltpu.VMEM((n_chunks, chunk, width), jnp.bfloat16),
            pltpu.SemaphoreType.DMA((2 * n_chunks,)),
        ],
        compiler_params=pltpu.CompilerParams(vmem_limit_bytes=ENC_BYTES),
        cost_estimate=pl.CostEstimate(
            flops=2 * rows * (2 * width * hidden + width * out_width),
            bytes_accessed=4 * width * hidden + 2 * rows * width,
            transcendentals=0,
        ),
        name="encode",
    )(hidden_in, up_weight, up_bias, down_weight, down_bias, norm_gain, norm_shift, proj_weight)


def body(
    hidden_in, up_weight, up_bias, down_weight, down_bias, norm_gain, norm_shift, proj_weight,
    centroids, lengths, owners, local_ids,
):
    n_devices = lax.axis_size("dp")
    token_rows = hidden_in.shape[0]
    width_out = proj_weight.shape[1]
    capacity = max(2, 2 * token_rows // n_devices)
    weights = (
        up_weight, up_bias, down_weight, down_bias, norm_gain, norm_shift, proj_weight,
    )
    slots, asked = plan(
        lengths, owners.reshape(-1, LANES), local_ids.reshape(-1, LANES), n_devices, capacity
    )
    arrived = lax.all_to_all(asked, "dp", split_axis=0, concat_axis=0, tiled=True)
    rows = gather_rows(arrived, centroids)
    hidden_in, rows = lax.optimization_barrier((hidden_in, rows))
    centers = lax.all_to_all(
        rows.reshape(n_devices, capacity, width_out), "dp", split_axis=0, concat_axis=0, tiled=True
    )
    embedded = encode(hidden_in, weights, 0, token_rows, 512, 768)
    centers, embedded = lax.optimization_barrier((centers, embedded))
    return finish(slots, embedded, centers.reshape(-1, width_out))


def solution(mesh):
    in_specs = (
        P(("groups", "dp"), None),
        P(),
        P(),
        P(),
        P(),
        P(),
        P(),
        P(),
        P("dp", None),
        P(("groups", "dp")),
        P(("groups", "dp"), None),
        P(("groups", "dp")),
    )
    out_specs = P(("groups", "dp"), None)
    return jax.shard_map(body, mesh=mesh, in_specs=in_specs, out_specs=out_specs, check_vma=False)
```

time: 52.6 us -> 41.3 us (0.79)
  blocking collectives: 0 us -> 13.8 us
  starting transfers between devices: 16.4 us -> 3.57 us
  Pallas kernels: 34.7 us -> 23.1 us
    all_to_all x0 -> x1, blocking collectives: none -> 13.8 us  [body(): lax.all_to_all(asked, 'dp', split_axis=0, concat_axis=0, tiled=True)]
    pallas_call x3 -> x2, Pallas kernels: 25.9 us -> 17.8 us  [the longest x1 15.3 us: encode(): pl.pallas_call(functools.partial(encode_kernel, tile_rows, chunk), in_spe...]
    all_to_all x1 -> x0, starting transfers between devices: 7.39 us -> none  [body(): lax.all_to_all(asked, 'dp', split_axis=0, concat_axis=0, tiled=True)]
    all_to_all x1, starting transfers between devices: 9.05 us -> 3.57 us  [body(): lax.all_to_all(rows.reshape(n_devices, capacity, width_out), 'dp', split_...]
    pallas_call x1, Pallas kernels: 7.18 us -> 3.55 us  [gather_rows(): pl.pallas_call(gather_kernel, in_specs=[SMEM, VMEM], out_specs=VMEM, out_...]
  transfers between devices with their start and end apart: 2 -> 1, of which waited for: 0 -> 0; matrix products, arithmetic and copies ran while one was open for 0% -> 0% of each run, Pallas kernels for 43% -> 37%
where the time goes in v3:
time: 41.3 us; the launch traced here: 41.5 us
  Pallas kernels  23.1 us (56%)
  blocking collectives  13.8 us (33%)
  starting transfers between devices  3.57 us (9%)
  local copies, waits for them, and re-layouts  0.95 us (2%)
    pallas_call x1, Pallas kernels, encode(): pl.pallas_call(functools.partial(encode_kernel, tile_rows, chunk), in_spe...  15.3 us
    all_to_all x1, blocking collectives, body(): lax.all_to_all(asked, 'dp', split_axis=0, concat_axis=0, tiled=True)  13.8 us
    all_to_all x1, starting transfers between devices, body(): lax.all_to_all(rows.reshape(n_devices, capacity, width_out), 'dp', split_...  3.57 us
    pallas_call x1, Pallas kernels, gather_rows(): pl.pallas_call(gather_kernel, in_specs=[SMEM, VMEM], out_specs=VMEM, out_...  3.55 us
    pallas_call x1, Pallas kernels, finish(): pl.pallas_call(finish_kernel, in_specs=[SMEM, VMEM, VMEM], out_specs=VMEM...  2.5 us
    pallas_call x1, Pallas kernels, plan(): pl.pallas_call(plan_kernel, in_specs=[SMEM, VMEM, VMEM], out_specs=[VMEM,...  1.75 us
    unnamed x16, local copies, waits for them, and re-layouts  0.95 us
  transfers between devices with their start and end apart: 1, of which 0 were waited for; matrix products, arithmetic and copies ran while one was open for 0% of the time, Pallas kernels for 37%

profile of v3, /device:TPU:0, one launch (start us, length us, event | category | flops | bytes accessed | tf_op | source)
XLA Modules:
  0.0 41.5 jit_solution(5500158364856866244)
XLA Ops:
  0.0 0.0 copy-start.2
  0.0 1.8 %plan.1 = (s32[16,128]{1,0:T(8,128)}, s32[16,128]{1,0:T(8,128)}) custom-call(s32[8]{0:T(128)} %lengths_ref.1, s32[8,128]{1,0:T(8,128)} %bitcast.11, s32[8,128]{1,0:T(8,128)} %bitcast.12), custom_call_target="tpu_custom_call" | custom-call | flops 20000000000 | bytes 1048576 | tf_op jit(solution)/shard_map/plan/pallas_call | solution.py:82
  1.8 13.8 %all_to_all.16 = s32[16,1,128]{2,1,0:T(1,128)S(1)} all-to-all(s32[16,1,128]{2,1,0:T(1,128)} %bitcast.10), channel_id=1, replica_groups=mesh['groups'=2,'dp'=16] {'dp'}, dimensions={0} | all-to-all | bytes 16384 | tf_op jit(solution)/shard_map/all_to_all | solution.py:292
  15.5 0.0 copy-done.2
  15.5 0.0 copy-start.1
  15.5 0.0 copy-start.4
  15.5 0.0 copy-start.5
  15.6 0.0 copy-start.6
  15.6 0.0 copy-start.7
  15.6 3.6 %gather_rows.1 = bf16[2048,128]{1,0:T(8,128)(2,1)} custom-call(s32[16,128]{1,0:T(8,128)S(1)} %bitcast.9, bf16[4096,128]{1,0:T(8,128)(2,1)S(1)} %copy-done.2), custom_call_target="tpu_custom_call" | custom-call | flops 20000000000 | bytes 1048576 | tf_op jit(solution)/shard_map/gather_rows/pallas_call | solution.py:123
  19.1 3.6 %all-to-all-start.1 = ((bf16[16,128,128]{2,1,0:T(8,128)(2,1)}), bf16[16,128,128]{2,1,0:T(8,128)(2,1)S(1)}, u32[]{:S(2)}, u32[]{:S(2)}) async-start(bf16[16,128,128]{2,1,0:T(8,128)(2,1)} %bitcast.5), calls=%async_computation.1 | async-start | bytes 1048576 | tf_op jit(solution)/shard_map/all_to_all | solution.py:295
  22.7 0.0 copy-done.1
  22.7 0.0 copy-done.4
  22.7 0.0 copy-done.5
  22.7 0.0 copy-done.6
  22.8 0.0 copy-done.7
  22.8 0.0 copy-start.3
  22.8 0.9 %copy-done.3 = bf16[768,128]{1,0:T(8,128)(2,1)S(1)} copy-done((bf16[768,128]{1,0:T(8,128)(2,1)S(1)}, bf16[768,128]{1,0:T(8,128)(2,1)}, u32[]{:S(2)}) %copy-start.3) | copy-done | bytes 196632
  23.7 0.0 copy-start
  23.7 15.3 %encode.1.embedded_ref = bf16[1024,128]{1,0:T(8,128)(2,1)S(1)} custom-call(bf16[1024,768]{1,0:T(8,128)(2,1)S(1)} %copy-done.1, bf16[768,3072]{1,0:T(8,128)(2,1)} %up_hbm.1, f32[3072]{0:T(1024)S(1)} %copy-done.4, bf16[3072,768]{1,0:T(8,128)(2,1)} %down_hbm.1, f32[768]{0:T(1024)S(1)} %copy-done.5, f32[768]{0:T(1024)S(1)} %copy-done.6, f32[768]{0:T(1024)S(1)} %copy-done.7, ...), custom_call_target="tpu_custom_call" | custom-call | flops 9865003008 | bytes 11010048 | tf_op jit(solution)/shard_map/encode/pallas_call | solution.py:258
  39.0 0.0 all-to-all-done.1
  39.0 0.0 copy-done
  39.0 2.5 %finish.1 = bf16[1024,128]{1,0:T(8,128)(2,1)} custom-call(s32[16,128]{1,0:T(8,128)S(1)} %copy-done, bf16[1024,128]{1,0:T(8,128)(2,1)S(1)} %encode.1.embedded_ref, bf16[2048,128]{1,0:T(8,128)(2,1)S(1)} %bitcast.8), custom_call_target="tpu_custom_call" | custom-call | tf_op jit(solution)/shard_map/finish/pallas_call | solution.py:169
Async XLA Ops:
  0.0 15.5 %copy-start.2 = (bf16[4096,128]{1,0:T(8,128)(2,1)S(1)}, bf16[4096,128]{1,0:T(8,128)(2,1)}, u32[]{:S(2)}) copy-start(bf16[4096,128]{1,0:T(8,128)(2,1)} %table_ref.1) | copy-start | bytes 3145732
  15.5 7.2 %copy-start.1 = (bf16[1024,768]{1,0:T(8,128)(2,1)S(1)}, bf16[1024,768]{1,0:T(8,128)(2,1)}, u32[]{:S(2)}) copy-start(bf16[1024,768]{1,0:T(8,128)(2,1)} %rows_ref) | copy-start | bytes 4718596
  15.5 7.2 %copy-start.4 = (f32[3072]{0:T(1024)S(1)}, f32[3072]{0:T(1024)}, u32[]{:S(2)}) copy-start(f32[3072]{0:T(1024)} %up_bias.1) | copy-start | bytes 36868
  15.5 7.2 %copy-start.5 = (f32[768]{0:T(1024)S(1)}, f32[768]{0:T(1024)}, u32[]{:S(2)}) copy-start(f32[768]{0:T(1024)} %down_bias.1) | copy-start | bytes 9220
  15.6 7.2 %copy-start.6 = (f32[768]{0:T(1024)S(1)}, f32[768]{0:T(1024)}, u32[]{:S(2)}) copy-start(f32[768]{0:T(1024)} %gain.1) | copy-start | bytes 9220
  15.6 7.2 %copy-start.7 = (f32[768]{0:T(1024)S(1)}, f32[768]{0:T(1024)}, u32[]{:S(2)}) copy-start(f32[768]{0:T(1024)} %shift.1) | copy-start | bytes 9220
  19.1 19.8 %all-to-all-start.1 = ((bf16[16,128,128]{2,1,0:T(8,128)(2,1)}), bf16[16,128,128]{2,1,0:T(8,128)(2,1)S(1)}, u32[]{:S(2)}, u32[]{:S(2)}) async-start(bf16[16,128,128]{2,1,0:T(8,128)(2,1)} %bitcast.5), calls=%async_computation.1 | async-start | bytes 1048576 | tf_op jit(solution)/shard_map/all_to_all | solution.py:295
  22.8 0.9 %copy-start.3 = (bf16[768,128]{1,0:T(8,128)(2,1)S(1)}, bf16[768,128]{1,0:T(8,128)(2,1)}, u32[]{:S(2)}) copy-start(bf16[768,128]{1,0:T(8,128)(2,1)} %proj.1) | copy-start | bytes 589828
  23.7 15.3 %copy-start = (s32[16,128]{1,0:T(8,128)S(1)}, s32[16,128]{1,0:T(8,128)}, u32[]{:S(2)}) copy-start(s32[16,128]{1,0:T(8,128)} %get-tuple-element.11.slots_ref) | copy-start | bytes 24580

commit v4 on v3

--- a/solution.py
+++ b/solution.py
@@ -14,11 +14,12 @@
 COUNT_SHIFT = 16
 BLOCK = 32
 VMEM_BYTES = 16 * 2**20
-ENC_BYTES = 48 * 2**20
+ENC_BYTES = 53 * 2**20
 AHEAD = 3
 VMEM = pl.BlockSpec(memory_space=pltpu.VMEM)
 SMEM = pl.BlockSpec(memory_space=pltpu.SMEM)
 HBM = pl.BlockSpec(memory_space=pltpu.HBM)
+ANY = pl.BlockSpec(memory_space=pl.ANY)
 
 
 def plan_kernel(lengths_ref, owners_ref, ids_ref, slots_ref, asked_ref):
@@ -92,8 +93,10 @@
     )(lengths, owners, local_ids)
 
 
-def gather_kernel(asked_ref, table_ref, out_ref, table_f32, out_f32):
+def gather_kernel(asked_hbm, table_ref, out_ref, asked_ref, table_f32, out_f32, arrived):
     n_owners, capacity = asked_ref.shape
+    asked_copy = pltpu.make_async_copy(asked_hbm, asked_ref, arrived)
+    asked_copy.start()
     table_f32[...] = table_ref[...].astype(jnp.float32)
 
     block = min(BLOCK, capacity)
@@ -113,6 +116,7 @@
 
         return carry
 
+    asked_copy.wait()
     lax.fori_loop(0, n_owners, device, 0)
     out_ref[...] = out_f32[...].astype(jnp.bfloat16)
 
@@ -122,12 +126,14 @@
     width = table.shape[1]
     return pl.pallas_call(
         gather_kernel,
-        in_specs=[SMEM, VMEM],
+        in_specs=[ANY, VMEM],
         out_specs=VMEM,
         out_shape=jax.ShapeDtypeStruct((rows, width), jnp.bfloat16),
         scratch_shapes=[
+            pltpu.SMEM(asked.shape, jnp.int32),
             pltpu.VMEM(table.shape, jnp.float32),
             pltpu.VMEM((rows, width), jnp.float32),
+            pltpu.SemaphoreType.DMA,
         ],
         compiler_params=pltpu.CompilerParams(vmem_limit_bytes=VMEM_BYTES),
         cost_estimate=pl.CostEstimate(flops=2 * 10**10, bytes_accessed=2**20, transcendentals=0),
@@ -135,7 +141,11 @@
     )(asked, table)
 
 
-def finish_kernel(slots_ref, embedded_ref, centers_ref, out_ref, centers_f32, mine):
+def finish_kernel(
+    slots_hbm, embedded_ref, centers_ref, out_ref, slots_ref, centers_f32, mine, arrived
+):
+    slots_copy = pltpu.make_async_copy(slots_hbm, slots_ref, arrived)
+    slots_copy.start()
     centers_f32[...] = centers_ref[...].astype(jnp.float32)
     n_passages = out_ref.shape[0] // LEN
 
@@ -152,6 +162,7 @@
 
         return carry
 
+    slots_copy.wait()
     lax.fori_loop(0, n_passages, passage_rows, 0)
     position = lax.broadcasted_iota(jnp.int32, (LEN, 1), 0)
     for passage in range(n_passages):
@@ -168,12 +179,14 @@
     width = centers.shape[1]
     return pl.pallas_call(
         finish_kernel,
-        in_specs=[SMEM, VMEM, VMEM],
+        in_specs=[ANY, VMEM, VMEM],
         out_specs=VMEM,
         out_shape=jax.ShapeDtypeStruct((rows, width), jnp.bfloat16),
         scratch_shapes=[
+            pltpu.SMEM(slots.shape, jnp.int32),
             pltpu.VMEM(centers.shape, jnp.float32),
             pltpu.VMEM((rows, width), jnp.float32),
+            pltpu.SemaphoreType.DMA,
         ],
         compiler_params=pltpu.CompilerParams(vmem_limit_bytes=VMEM_BYTES),
         name="finish",
@@ -181,8 +194,8 @@
 
 
 def encode_kernel(
-    tile_rows, chunk, rows_ref, up_hbm, up_bias, down_hbm, down_bias, gain, shift, proj, out_ref,
-    up_vmem, down_vmem, arrived,
+    first_rows, later_rows, chunk, rows_hbm, up_hbm, up_bias, down_hbm, down_bias, gain, shift, proj, out_ref,
+    rows_vmem, up_vmem, down_vmem, arrived,
 ):
     n_chunks = up_vmem.shape[0]
     queue = []
@@ -195,14 +208,22 @@
             ),
         ]
 
+    def rows_copy(start, count, semaphore):
+        at = pl.ds(start, count)
+        return pltpu.make_async_copy(rows_hbm.at[at, :], rows_vmem.at[at, :], semaphore)
+
+    n_rows = out_ref.shape[0]
+    rows_first = rows_copy(0, first_rows, arrived.at[2 * n_chunks])
+    queue.append(rows_copy(first_rows, n_rows - first_rows, arrived.at[2 * n_chunks + 1]))
+
     def wait_weights(index):
         queue[index].wait()
         for copy in queue[index + AHEAD : index + AHEAD + 1]:
             copy.start()
 
-    def tile(start, first):
-        at = pl.ds(start, tile_rows)
-        rows = rows_ref[at, :]
+    def tile(start, count, first):
+        at = pl.ds(start, count)
+        rows = rows_vmem[at, :]
 
         def up(index):
             return (
@@ -239,31 +260,37 @@
         size = jnp.sum(projected * projected, axis=1, keepdims=True)
         out_ref[at, :] = (projected * lax.rsqrt(size + 1e-06)).astype(jnp.bfloat16)
 
+    rows_first.start()
     for copy in queue[:AHEAD]:
         copy.start()
-    tile(0, True)
+    rows_first.wait()
+    tile(0, first_rows, True)
+    wait_weights(2 * n_chunks)
 
     def later(index, carry):
-        tile(pl.multiple_of(index * tile_rows, tile_rows), False)
+        start = pl.multiple_of(first_rows + index * later_rows, LANES)
+        tile(start, later_rows, False)
         return carry
 
-    lax.fori_loop(1, out_ref.shape[0] // tile_rows, later, 0)
-
-
-def encode(hidden_in, weights, start, rows, tile_rows, chunk):
+    lax.fori_loop(0, (n_rows - first_rows) // later_rows, later, 0)
+
+
+def encode(hidden_in, weights, first_rows, later_rows, chunk):
+    rows = hidden_in.shape[0]
     up_weight, up_bias, down_weight, down_bias, norm_gain, norm_shift, proj_weight = weights
     width, hidden = up_weight.shape
     out_width = proj_weight.shape[1]
     n_chunks = hidden // chunk
     return pl.pallas_call(
-        functools.partial(encode_kernel, tile_rows, chunk),
-        in_specs=[VMEM, HBM, VMEM, HBM, VMEM, VMEM, VMEM, VMEM],
+        functools.partial(encode_kernel, first_rows, later_rows, chunk),
+        in_specs=[HBM, HBM, VMEM, HBM, VMEM, VMEM, VMEM, VMEM],
         out_specs=VMEM,
         out_shape=jax.ShapeDtypeStruct((rows, out_width), jnp.bfloat16),
         scratch_shapes=[
+            pltpu.VMEM((rows, width), jnp.bfloat16),
             pltpu.VMEM((n_chunks, width, chunk), jnp.bfloat16),
             pltpu.VMEM((n_chunks, chunk, width), jnp.bfloat16),
-            pltpu.SemaphoreType.DMA((2 * n_chunks,)),
+            pltpu.SemaphoreType.DMA((2 * n_chunks + 2,)),
         ],
         compiler_params=pltpu.CompilerParams(vmem_limit_bytes=ENC_BYTES),
         cost_estimate=pl.CostEstimate(
@@ -295,7 +322,7 @@
     centers = lax.all_to_all(
         rows.reshape(n_devices, capacity, width_out), "dp", split_axis=0, concat_axis=0, tiled=True
     )
-    embedded = encode(hidden_in, weights, 0, token_rows, 512, 768)
+    embedded = encode(hidden_in, weights, 256, 768, 768)
     centers, embedded = lax.optimization_barrier((centers, embedded))
     return finish(slots, embedded, centers.reshape(-1, width_out))
 

time: 41.3 us -> 39.9 us (0.966)
  local copies, waits for them, and re-layouts: 0.95 us -> 0.03 us
  Pallas kernels: 23.1 us -> 22.2 us
    unnamed x16 -> x14, local copies, waits for them, and re-layouts: 0.95 us -> 0.03 us
    pallas_call x3, Pallas kernels: 21.3 us -> 20.4 us  [the longest x1 15.3 us: encode(): pl.pallas_call(functools.partial(encode_kernel, first_rows, later_rows, c...]
  transfers between devices with their start and end apart: 1 -> 1, of which waited for: 0 -> 0; matrix products, arithmetic and copies ran while one was open for 0% -> 0% of each run, Pallas kernels for 37% -> 39%
where the time goes in v4:
time: 39.9 us; the launch traced here: 39.7 us
  Pallas kernels  22.2 us (56%)
  blocking collectives  13.8 us (35%)
  starting transfers between devices  3.58 us (9%)
    pallas_call x1, Pallas kernels, encode(): pl.pallas_call(functools.partial(encode_kernel, first_rows, later_rows, c...  15.3 us
    all_to_all x1, blocking collectives, body(): lax.all_to_all(asked, 'dp', split_axis=0, concat_axis=0, tiled=True)  13.8 us
    all_to_all x1, starting transfers between devices, body(): lax.all_to_all(rows.reshape(n_devices, capacity, width_out), 'dp', split_...  3.58 us
    pallas_call x1, Pallas kernels, finish(): pl.pallas_call(finish_kernel, in_specs=[ANY, VMEM, VMEM], out_specs=VMEM,...  2.59 us
    pallas_call x1, Pallas kernels, gather_rows(): pl.pallas_call(gather_kernel, in_specs=[ANY, VMEM], out_specs=VMEM, out_s...  2.52 us
    pallas_call x1, Pallas kernels, plan(): pl.pallas_call(plan_kernel, in_specs=[SMEM, VMEM, VMEM], out_specs=[VMEM,...  1.76 us
  transfers between devices with their start and end apart: 1, of which 0 were waited for; matrix products, arithmetic and copies ran while one was open for 0% of the time, Pallas kernels for 39%

profile of v4, /device:TPU:0, one launch (start us, length us, event | category | flops | bytes accessed | tf_op | source)
XLA Modules:
  0.0 39.7 jit_solution(5881619147022608144)
XLA Ops:
  0.0 0.0 copy-start.1
  0.0 1.8 %plan.1 = (s32[16,128]{1,0:T(8,128)}, s32[16,128]{1,0:T(8,128)}) custom-call(s32[8]{0:T(128)} %lengths_ref.1, s32[8,128]{1,0:T(8,128)} %bitcast.11, s32[8,128]{1,0:T(8,128)} %bitcast.12), custom_call_target="tpu_custom_call" | custom-call | flops 20000000000 | bytes 1048576 | tf_op jit(solution)/shard_map/plan/pallas_call | solution.py:83
  1.8 13.8 %all_to_all.16 = s32[16,1,128]{2,1,0:T(1,128)S(1)} all-to-all(s32[16,1,128]{2,1,0:T(1,128)} %bitcast.10), channel_id=1, replica_groups=mesh['groups'=2,'dp'=16] {'dp'}, dimensions={0} | all-to-all | bytes 16384 | tf_op jit(solution)/shard_map/all_to_all | solution.py:319
  15.6 0.0 copy-done.1
  15.6 0.0 copy-start.2
  15.6 0.0 copy-start.3
  15.6 0.0 copy-start.4
  15.6 0.0 copy-start.5
  15.6 0.0 copy-start.6
  15.6 2.5 %gather_rows.1 = bf16[2048,128]{1,0:T(8,128)(2,1)} custom-call(s32[16,128]{1,0:T(8,128)S(1)} %bitcast.9, bf16[4096,128]{1,0:T(8,128)(2,1)S(1)} %copy-done.1), custom_call_target="tpu_custom_call" | custom-call | flops 20000000000 | bytes 1048576 | tf_op jit(solution)/shard_map/gather_rows/pallas_call | solution.py:127
  18.1 3.6 %all-to-all-start.1 = ((bf16[16,128,128]{2,1,0:T(8,128)(2,1)}), bf16[16,128,128]{2,1,0:T(8,128)(2,1)S(1)}, u32[]{:S(2)}, u32[]{:S(2)}) async-start(bf16[16,128,128]{2,1,0:T(8,128)(2,1)} %bitcast.5), calls=%async_computation.1 | async-start | bytes 1048576 | tf_op jit(solution)/shard_map/all_to_all | solution.py:322
  21.7 0.0 copy-done.2
  21.7 0.0 copy-done.3
  21.7 0.0 copy-done.4
  21.7 0.0 copy-done.5
  21.7 0.0 copy-done.6
  21.8 0.0 copy-start
  21.8 15.3 %encode.1.embedded_ref = bf16[1024,128]{1,0:T(8,128)(2,1)S(1)} custom-call(bf16[1024,768]{1,0:T(8,128)(2,1)} %rows_hbm, bf16[768,3072]{1,0:T(8,128)(2,1)} %up_hbm.1, f32[3072]{0:T(1024)S(1)} %copy-done.3, bf16[3072,768]{1,0:T(8,128)(2,1)} %down_hbm.1, f32[768]{0:T(1024)S(1)} %copy-done.4, f32[768]{0:T(1024)S(1)} %copy-done.5, f32[768]{0:T(1024)S(1)} %copy-done.6, ...), custom_call_target="tpu_custom_call" | custom-call | flops 9865003008 | bytes 11010048 | tf_op jit(solution)/shard_map/encode/pallas_call | solution.py:284
  37.1 0.0 all-to-all-done.1
  37.1 0.0 copy-done
  37.1 2.6 %finish.1 = bf16[1024,128]{1,0:T(8,128)(2,1)} custom-call(s32[16,128]{1,0:T(8,128)S(1)} %copy-done, bf16[1024,128]{1,0:T(8,128)(2,1)S(1)} %encode.1.embedded_ref, bf16[2048,128]{1,0:T(8,128)(2,1)S(1)} %bitcast.8), custom_call_target="tpu_custom_call" | custom-call | tf_op jit(solution)/shard_map/finish/pallas_call | solution.py:180
Async XLA Ops:
  0.0 15.6 %copy-start.1 = (bf16[4096,128]{1,0:T(8,128)(2,1)S(1)}, bf16[4096,128]{1,0:T(8,128)(2,1)}, u32[]{:S(2)}) copy-start(bf16[4096,128]{1,0:T(8,128)(2,1)} %table_ref.1) | copy-start | bytes 3145732
  15.6 6.2 %copy-start.2 = (bf16[768,128]{1,0:T(8,128)(2,1)S(1)}, bf16[768,128]{1,0:T(8,128)(2,1)}, u32[]{:S(2)}) copy-start(bf16[768,128]{1,0:T(8,128)(2,1)} %proj.1) | copy-start | bytes 589828
  15.6 6.2 %copy-start.3 = (f32[3072]{0:T(1024)S(1)}, f32[3072]{0:T(1024)}, u32[]{:S(2)}) copy-start(f32[3072]{0:T(1024)} %up_bias.1) | copy-start | bytes 36868
  15.6 6.2 %copy-start.4 = (f32[768]{0:T(1024)S(1)}, f32[768]{0:T(1024)}, u32[]{:S(2)}) copy-start(f32[768]{0:T(1024)} %down_bias.1) | copy-start | bytes 9220
  15.6 6.2 %copy-start.5 = (f32[768]{0:T(1024)S(1)}, f32[768]{0:T(1024)}, u32[]{:S(2)}) copy-start(f32[768]{0:T(1024)} %gain.1) | copy-start | bytes 9220
  15.6 6.2 %copy-start.6 = (f32[768]{0:T(1024)S(1)}, f32[768]{0:T(1024)}, u32[]{:S(2)}) copy-start(f32[768]{0:T(1024)} %shift.1) | copy-start | bytes 9220
  18.1 19.0 %all-to-all-start.1 = ((bf16[16,128,128]{2,1,0:T(8,128)(2,1)}), bf16[16,128,128]{2,1,0:T(8,128)(2,1)S(1)}, u32[]{:S(2)}, u32[]{:S(2)}) async-start(bf16[16,128,128]{2,1,0:T(8,128)(2,1)} %bitcast.5), calls=%async_computation.1 | async-start | bytes 1048576 | tf_op jit(solution)/shard_map/all_to_all | solution.py:322
  21.8 15.3 %copy-start = (s32[16,128]{1,0:T(8,128)S(1)}, s32[16,128]{1,0:T(8,128)}, u32[]{:S(2)}) copy-start(s32[16,128]{1,0:T(8,128)} %get-tuple-element.11.slots_hbm) | copy-start | bytes 24580

commit v5 on v4

--- a/solution.py
+++ b/solution.py
@@ -15,7 +15,8 @@
 BLOCK = 32
 VMEM_BYTES = 16 * 2**20
 ENC_BYTES = 53 * 2**20
-AHEAD = 3
+AHEAD = 10
+FIRST_CHUNK = 256
 VMEM = pl.BlockSpec(memory_space=pltpu.VMEM)
 SMEM = pl.BlockSpec(memory_space=pltpu.SMEM)
 HBM = pl.BlockSpec(memory_space=pltpu.HBM)
@@ -197,15 +198,17 @@
     first_rows, later_rows, chunk, rows_hbm, up_hbm, up_bias, down_hbm, down_bias, gain, shift, proj, out_ref,
     rows_vmem, up_vmem, down_vmem, arrived,
 ):
-    n_chunks = up_vmem.shape[0]
+    hidden = up_vmem.shape[1]
+    later_bounds = list(range(0, hidden + 1, chunk))
+    first_bounds = [0, FIRST_CHUNK] + later_bounds[1:]
+    n_copies = 2 * (len(first_bounds) - 1)
     queue = []
-    for index in range(n_chunks):
-        at = pl.ds(index * chunk, chunk)
+    for low, high in zip(first_bounds, first_bounds[1:]):
+        at = pl.ds(low, high - low)
+        semaphores = [arrived.at[len(queue)], arrived.at[len(queue) + 1]]
         queue += [
-            pltpu.make_async_copy(up_hbm.at[:, at], up_vmem.at[index], arrived.at[2 * index]),
-            pltpu.make_async_copy(
-                down_hbm.at[at, :], down_vmem.at[index], arrived.at[2 * index + 1]
-            ),
+            pltpu.make_async_copy(up_hbm.at[:, at], up_vmem.at[:, at], semaphores[0]),
+            pltpu.make_async_copy(down_hbm.at[at, :], down_vmem.at[at, :], semaphores[1]),
         ]
 
     def rows_copy(start, count, semaphore):
@@ -213,8 +216,8 @@
         return pltpu.make_async_copy(rows_hbm.at[at, :], rows_vmem.at[at, :], semaphore)
 
     n_rows = out_ref.shape[0]
-    rows_first = rows_copy(0, first_rows, arrived.at[2 * n_chunks])
-    queue.append(rows_copy(first_rows, n_rows - first_rows, arrived.at[2 * n_chunks + 1]))
+    rows_first = rows_copy(0, first_rows, arrived.at[n_copies])
+    queue.append(rows_copy(first_rows, n_rows - first_rows, arrived.at[n_copies + 1]))
 
     def wait_weights(index):
         queue[index].wait()
@@ -225,10 +228,14 @@
         at = pl.ds(start, count)
         rows = rows_vmem[at, :]
 
+        bounds = first_bounds if first else later_bounds
+        n_chunks = len(bounds) - 1
+
         def up(index):
+            part = slice(bounds[index], bounds[index + 1])
             return (
-                jnp.dot(rows, up_vmem[index], preferred_element_type=jnp.float32)
-                + up_bias[index * chunk : (index + 1) * chunk][None, :]
+                jnp.dot(rows, up_vmem[:, part], preferred_element_type=jnp.float32)
+                + up_bias[part][None, :]
             )
 
         total = None
@@ -246,7 +253,11 @@
             activated = (0.5 * up_proj * (1.0 + lax.erf(up_proj * 0.7071067811865476))).astype(
                 jnp.bfloat16
             )
-            part = jnp.dot(activated, down_vmem[index], preferred_element_type=jnp.float32)
+            part = jnp.dot(
+                activated,
+                down_vmem[bounds[index] : bounds[index + 1], :],
+                preferred_element_type=jnp.float32,
+            )
             total = part if total is None else total + part
             up_proj = following
         ffn_out = total + down_bias[...][None, :] + rows.astype(jnp.float32)
@@ -265,7 +276,7 @@
         copy.start()
     rows_first.wait()
     tile(0, first_rows, True)
-    wait_weights(2 * n_chunks)
+    wait_weights(n_copies)
 
     def later(index, carry):
         start = pl.multiple_of(first_rows + index * later_rows, LANES)
@@ -280,7 +291,7 @@
     up_weight, up_bias, down_weight, down_bias, norm_gain, norm_shift, proj_weight = weights
     width, hidden = up_weight.shape
     out_width = proj_weight.shape[1]
-    n_chunks = hidden // chunk
+    n_copies = 2 * (hidden // chunk + 1)
     return pl.pallas_call(
         functools.partial(encode_kernel, first_rows, later_rows, chunk),
         in_specs=[HBM, HBM, VMEM, HBM, VMEM, VMEM, VMEM, VMEM],
@@ -288,9 +299,9 @@
         out_shape=jax.ShapeDtypeStruct((rows, out_width), jnp.bfloat16),
         scratch_shapes=[
             pltpu.VMEM((rows, width), jnp.bfloat16),
-            pltpu.VMEM((n_chunks, width, chunk), jnp.bfloat16),
-            pltpu.VMEM((n_chunks, chunk, width), jnp.bfloat16),
-            pltpu.SemaphoreType.DMA((2 * n_chunks + 2,)),
+            pltpu.VMEM((width, hidden), jnp.bfloat16),
+            pltpu.VMEM((hidden, width), jnp.bfloat16),
+            pltpu.SemaphoreType.DMA((n_copies + 2,)),
         ],
         compiler_params=pltpu.CompilerParams(vmem_limit_bytes=ENC_BYTES),
         cost_estimate=pl.CostEstimate(

time: 39.9 us -> 39.4 us (0.987)
  Pallas kernels: 22.2 us -> 21.5 us
    pallas_call x1, Pallas kernels: 15.3 us -> 14.4 us  [encode(): pl.pallas_call(functools.partial(encode_kernel, first_rows, later_rows, c...]
  transfers between devices with their start and end apart: 1 -> 1, of which waited for: 0 -> 0; matrix products, arithmetic and copies ran while one was open for 0% -> 0% of each run, Pallas kernels for 39% -> 37%
where the time goes in v5:
time: 39.4 us; the launch traced here: 39 us
  Pallas kernels  21.5 us (55%)
  blocking collectives  13.8 us (35%)
  starting transfers between devices  3.58 us (9%)
    pallas_call x1, Pallas kernels, encode(): pl.pallas_call(functools.partial(encode_kernel, first_rows, later_rows, c...  14.4 us
    all_to_all x1, blocking collectives, body(): lax.all_to_all(asked, 'dp', split_axis=0, concat_axis=0, tiled=True)  13.8 us
    all_to_all x1, starting transfers between devices, body(): lax.all_to_all(rows.reshape(n_devices, capacity, width_out), 'dp', split_...  3.58 us
    pallas_call x1, Pallas kernels, gather_rows(): pl.pallas_call(gather_kernel, in_specs=[ANY, VMEM], out_specs=VMEM, out_s...  2.71 us
    pallas_call x1, Pallas kernels, finish(): pl.pallas_call(finish_kernel, in_specs=[ANY, VMEM, VMEM], out_specs=VMEM,...  2.56 us
    pallas_call x1, Pallas kernels, plan(): pl.pallas_call(plan_kernel, in_specs=[SMEM, VMEM, VMEM], out_specs=[VMEM,...  1.76 us
  transfers between devices with their start and end apart: 1, of which 0 were waited for; matrix products, arithmetic and copies ran while one was open for 0% of the time, Pallas kernels for 37%

profile of v5, /device:TPU:0, one launch (start us, length us, event | category | flops | bytes accessed | tf_op | source)
XLA Modules:
  0.0 39.0 jit_solution(5259337857185692357)
XLA Ops:
  0.0 0.0 copy-start.1
  0.0 1.8 %plan.1 = (s32[16,128]{1,0:T(8,128)}, s32[16,128]{1,0:T(8,128)}) custom-call(s32[8]{0:T(128)} %lengths_ref.1, s32[8,128]{1,0:T(8,128)} %bitcast.11, s32[8,128]{1,0:T(8,128)} %bitcast.12), custom_call_target="tpu_custom_call" | custom-call | flops 20000000000 | bytes 1048576 | tf_op jit(solution)/shard_map/plan/pallas_call | solution.py:84
  1.8 13.8 %all_to_all.16 = s32[16,1,128]{2,1,0:T(1,128)S(1)} all-to-all(s32[16,1,128]{2,1,0:T(1,128)} %bitcast.10), channel_id=1, replica_groups=mesh['groups'=2,'dp'=16] {'dp'}, dimensions={0} | all-to-all | bytes 16384 | tf_op jit(solution)/shard_map/all_to_all | solution.py:330
  15.6 0.0 copy-done.1
  15.6 0.0 copy-start.2
  15.6 0.0 copy-start.3
  15.6 0.0 copy-start.4
  15.6 0.0 copy-start.5
  15.6 0.0 copy-start.6
  15.6 2.7 %gather_rows.1 = bf16[2048,128]{1,0:T(8,128)(2,1)} custom-call(s32[16,128]{1,0:T(8,128)S(1)} %bitcast.9, bf16[4096,128]{1,0:T(8,128)(2,1)S(1)} %copy-done.1), custom_call_target="tpu_custom_call" | custom-call | flops 20000000000 | bytes 1048576 | tf_op jit(solution)/shard_map/gather_rows/pallas_call | solution.py:128
  18.3 3.6 %all-to-all-start.1 = ((bf16[16,128,128]{2,1,0:T(8,128)(2,1)}), bf16[16,128,128]{2,1,0:T(8,128)(2,1)S(1)}, u32[]{:S(2)}, u32[]{:S(2)}) async-start(bf16[16,128,128]{2,1,0:T(8,128)(2,1)} %bitcast.5), calls=%async_computation.1 | async-start | bytes 1048576 | tf_op jit(solution)/shard_map/all_to_all | solution.py:333
  21.9 0.0 copy-done.2
  21.9 0.0 copy-done.3
  21.9 0.0 copy-done.4
  21.9 0.0 copy-done.5
  21.9 0.0 copy-done.6
  22.0 0.0 copy-start
  22.0 14.4 %encode.1.embedded_ref = bf16[1024,128]{1,0:T(8,128)(2,1)S(1)} custom-call(bf16[1024,768]{1,0:T(8,128)(2,1)} %rows_hbm, bf16[768,3072]{1,0:T(8,128)(2,1)} %up_hbm.1, f32[3072]{0:T(1024)S(1)} %copy-done.3, bf16[3072,768]{1,0:T(8,128)(2,1)} %down_hbm.1, f32[768]{0:T(1024)S(1)} %copy-done.4, f32[768]{0:T(1024)S(1)} %copy-done.5, f32[768]{0:T(1024)S(1)} %copy-done.6, ...), custom_call_target="tpu_custom_call" | custom-call | flops 9865003008 | bytes 11010048 | tf_op jit(solution)/shard_map/encode/pallas_call | solution.py:295
  36.4 0.0 all-to-all-done.1
  36.4 0.0 copy-done
  36.4 2.6 %finish.1 = bf16[1024,128]{1,0:T(8,128)(2,1)} custom-call(s32[16,128]{1,0:T(8,128)S(1)} %copy-done, bf16[1024,128]{1,0:T(8,128)(2,1)S(1)} %encode.1.embedded_ref, bf16[2048,128]{1,0:T(8,128)(2,1)S(1)} %bitcast.8), custom_call_target="tpu_custom_call" | custom-call | tf_op jit(solution)/shard_map/finish/pallas_call | solution.py:181
Async XLA Ops:
  0.0 15.6 %copy-start.1 = (bf16[4096,128]{1,0:T(8,128)(2,1)S(1)}, bf16[4096,128]{1,0:T(8,128)(2,1)}, u32[]{:S(2)}) copy-start(bf16[4096,128]{1,0:T(8,128)(2,1)} %table_ref.1) | copy-start | bytes 3145732
  15.6 6.3 %copy-start.2 = (bf16[768,128]{1,0:T(8,128)(2,1)S(1)}, bf16[768,128]{1,0:T(8,128)(2,1)}, u32[]{:S(2)}) copy-start(bf16[768,128]{1,0:T(8,128)(2,1)} %proj.1) | copy-start | bytes 589828
  15.6 6.4 %copy-start.3 = (f32[3072]{0:T(1024)S(1)}, f32[3072]{0:T(1024)}, u32[]{:S(2)}) copy-start(f32[3072]{0:T(1024)} %up_bias.1) | copy-start | bytes 36868
  15.6 6.4 %copy-start.4 = (f32[768]{0:T(1024)S(1)}, f32[768]{0:T(1024)}, u32[]{:S(2)}) copy-start(f32[768]{0:T(1024)} %down_bias.1) | copy-start | bytes 9220
  15.6 6.4 %copy-start.5 = (f32[768]{0:T(1024)S(1)}, f32[768]{0:T(1024)}, u32[]{:S(2)}) copy-start(f32[768]{0:T(1024)} %gain.1) | copy-start | bytes 9220
  15.6 6.4 %copy-start.6 = (f32[768]{0:T(1024)S(1)}, f32[768]{0:T(1024)}, u32[]{:S(2)}) copy-start(f32[768]{0:T(1024)} %shift.1) | copy-start | bytes 9220
  18.3 18.1 %all-to-all-start.1 = ((bf16[16,128,128]{2,1,0:T(8,128)(2,1)}), bf16[16,128,128]{2,1,0:T(8,128)(2,1)S(1)}, u32[]{:S(2)}, u32[]{:S(2)}) async-start(bf16[16,128,128]{2,1,0:T(8,128)(2,1)} %bitcast.5), calls=%async_computation.1 | async-start | bytes 1048576 | tf_op jit(solution)/shard_map/all_to_all | solution.py:333
  22.0 14.5 %copy-start = (s32[16,128]{1,0:T(8,128)S(1)}, s32[16,128]{1,0:T(8,128)}, u32[]{:S(2)}) copy-start(s32[16,128]{1,0:T(8,128)} %get-tuple-element.11.slots_hbm) | copy-start | bytes 24580

commit v6 on v5

--- a/solution.py
+++ b/solution.py
@@ -247,9 +247,7 @@
                 wait_weights(2 * index + 1)
                 if index + 1 < n_chunks:
                     wait_weights(2 * index + 2)
-            following = up(index + 1) if first and index + 1 < n_chunks else None
-            if not first and index > 0:
-                up_proj = up(index)
+            following = up(index + 1) if index + 1 < n_chunks else None
             activated = (0.5 * up_proj * (1.0 + lax.erf(up_proj * 0.7071067811865476))).astype(
                 jnp.bfloat16
             )

time: 39.4 us -> 39 us (0.990)
  transfers between devices with their start and end apart: 1 -> 1, of which waited for: 0 -> 1; matrix products, arithmetic and copies ran while one was open for 0% -> 0% of each run, Pallas kernels for 37% -> 37%
where the time goes in v6:
time: 39 us; the launch traced here: 38.8 us
  Pallas kernels  21.2 us (54%)
  blocking collectives  13.8 us (35%)
  starting transfers between devices  3.58 us (9%)
    pallas_call x1, Pallas kernels, encode(): pl.pallas_call(functools.partial(encode_kernel, first_rows, later_rows, c...  14.2 us
    all_to_all x1, blocking collectives, body(): lax.all_to_all(asked, 'dp', split_axis=0, concat_axis=0, tiled=True)  13.8 us
    all_to_all x1, starting transfers between devices, body(): lax.all_to_all(rows.reshape(n_devices, capacity, width_out), 'dp', split_...  3.58 us
    pallas_call x1, Pallas kernels, finish(): pl.pallas_call(finish_kernel, in_specs=[ANY, VMEM, VMEM], out_specs=VMEM,...  2.64 us
    pallas_call x1, Pallas kernels, gather_rows(): pl.pallas_call(gather_kernel, in_specs=[ANY, VMEM], out_specs=VMEM, out_s...  2.54 us
    pallas_call x1, Pallas kernels, plan(): pl.pallas_call(plan_kernel, in_specs=[SMEM, VMEM, VMEM], out_specs=[VMEM,...  1.76 us
  transfers between devices with their start and end apart: 1, of which 1 were waited for; matrix products, arithmetic and copies ran while one was open for 0% of the time, Pallas kernels for 37%

profile of v6, /device:TPU:0, one launch (start us, length us, event | category | flops | bytes accessed | tf_op | source)
XLA Modules:
  0.0 38.8 jit_solution(7884278564491178376)
XLA Ops:
  0.0 0.0 copy-start.1
  0.0 1.8 %plan.1 = (s32[16,128]{1,0:T(8,128)}, s32[16,128]{1,0:T(8,128)}) custom-call(s32[8]{0:T(128)} %lengths_ref.1, s32[8,128]{1,0:T(8,128)} %bitcast.11, s32[8,128]{1,0:T(8,128)} %bitcast.12), custom_call_target="tpu_custom_call" | custom-call | flops 20000000000 | bytes 1048576 | tf_op jit(solution)/shard_map/plan/pallas_call | solution.py:84
  1.8 13.8 %all_to_all.16 = s32[16,1,128]{2,1,0:T(1,128)S(1)} all-to-all(s32[16,1,128]{2,1,0:T(1,128)} %bitcast.10), channel_id=1, replica_groups=mesh['groups'=2,'dp'=16] {'dp'}, dimensions={0} | all-to-all | bytes 16384 | tf_op jit(solution)/shard_map/all_to_all | solution.py:328
  15.6 0.0 copy-done.1
  15.6 0.0 copy-start.2
  15.6 0.0 copy-start.3
  15.6 0.0 copy-start.4
  15.6 0.0 copy-start.5
  15.6 0.0 copy-start.6
  15.6 2.5 %gather_rows.1 = bf16[2048,128]{1,0:T(8,128)(2,1)} custom-call(s32[16,128]{1,0:T(8,128)S(1)} %bitcast.9, bf16[4096,128]{1,0:T(8,128)(2,1)S(1)} %copy-done.1), custom_call_target="tpu_custom_call" | custom-call | flops 20000000000 | bytes 1048576 | tf_op jit(solution)/shard_map/gather_rows/pallas_call | solution.py:128
  18.1 3.6 %all-to-all-start.1 = ((bf16[16,128,128]{2,1,0:T(8,128)(2,1)}), bf16[16,128,128]{2,1,0:T(8,128)(2,1)S(1)}, u32[]{:S(2)}, u32[]{:S(2)}) async-start(bf16[16,128,128]{2,1,0:T(8,128)(2,1)} %bitcast.5), calls=%async_computation.1 | async-start | bytes 1048576 | tf_op jit(solution)/shard_map/all_to_all | solution.py:331
  21.7 0.0 copy-done.2
  21.7 0.0 copy-done.3
  21.8 0.0 copy-done.4
  21.8 0.0 copy-done.5
  21.8 0.0 copy-done.6
  21.8 0.0 copy-start
  21.8 14.2 %encode.1.embedded_ref = bf16[1024,128]{1,0:T(8,128)(2,1)S(1)} custom-call(bf16[1024,768]{1,0:T(8,128)(2,1)} %rows_hbm, bf16[768,3072]{1,0:T(8,128)(2,1)} %up_hbm.1, f32[3072]{0:T(1024)S(1)} %copy-done.3, bf16[3072,768]{1,0:T(8,128)(2,1)} %down_hbm.1, f32[768]{0:T(1024)S(1)} %copy-done.4, f32[768]{0:T(1024)S(1)} %copy-done.5, f32[768]{0:T(1024)S(1)} %copy-done.6, ...), custom_call_target="tpu_custom_call" | custom-call | flops 9865003008 | bytes 11010048 | tf_op jit(solution)/shard_map/encode/pallas_call | solution.py:293
  36.0 0.1 all-to-all-done.1
  36.2 0.0 copy-done
  36.2 2.6 %finish.1 = bf16[1024,128]{1,0:T(8,128)(2,1)} custom-call(s32[16,128]{1,0:T(8,128)S(1)} %copy-done, bf16[1024,128]{1,0:T(8,128)(2,1)S(1)} %encode.1.embedded_ref, bf16[2048,128]{1,0:T(8,128)(2,1)S(1)} %bitcast.8), custom_call_target="tpu_custom_call" | custom-call | tf_op jit(solution)/shard_map/finish/pallas_call | solution.py:181
Async XLA Ops:
  0.0 15.6 %copy-start.1 = (bf16[4096,128]{1,0:T(8,128)(2,1)S(1)}, bf16[4096,128]{1,0:T(8,128)(2,1)}, u32[]{:S(2)}) copy-start(bf16[4096,128]{1,0:T(8,128)(2,1)} %table_ref.1) | copy-start | bytes 3145732
  15.6 6.2 %copy-start.2 = (bf16[768,128]{1,0:T(8,128)(2,1)S(1)}, bf16[768,128]{1,0:T(8,128)(2,1)}, u32[]{:S(2)}) copy-start(bf16[768,128]{1,0:T(8,128)(2,1)} %proj.1) | copy-start | bytes 589828
  15.6 6.2 %copy-start.3 = (f32[3072]{0:T(1024)S(1)}, f32[3072]{0:T(1024)}, u32[]{:S(2)}) copy-start(f32[3072]{0:T(1024)} %up_bias.1) | copy-start | bytes 36868
  15.6 6.2 %copy-start.4 = (f32[768]{0:T(1024)S(1)}, f32[768]{0:T(1024)}, u32[]{:S(2)}) copy-start(f32[768]{0:T(1024)} %down_bias.1) | copy-start | bytes 9220
  15.6 6.2 %copy-start.5 = (f32[768]{0:T(1024)S(1)}, f32[768]{0:T(1024)}, u32[]{:S(2)}) copy-start(f32[768]{0:T(1024)} %gain.1) | copy-start | bytes 9220
  15.6 6.2 %copy-start.6 = (f32[768]{0:T(1024)S(1)}, f32[768]{0:T(1024)}, u32[]{:S(2)}) copy-start(f32[768]{0:T(1024)} %shift.1) | copy-start | bytes 9220
  18.1 18.0 %all-to-all-start.1 = ((bf16[16,128,128]{2,1,0:T(8,128)(2,1)}), bf16[16,128,128]{2,1,0:T(8,128)(2,1)S(1)}, u32[]{:S(2)}, u32[]{:S(2)}) async-start(bf16[16,128,128]{2,1,0:T(8,128)(2,1)} %bitcast.5), calls=%async_computation.1 | async-start | bytes 1048576 | tf_op jit(solution)/shard_map/all_to_all | solution.py:331
  21.8 14.4 %copy-start = (s32[16,128]{1,0:T(8,128)S(1)}, s32[16,128]{1,0:T(8,128)}, u32[]{:S(2)}) copy-start(s32[16,128]{1,0:T(8,128)} %get-tuple-element.11.slots_hbm) | copy-start | bytes 24580
